TPU v7x, 768 devices: a whole 4x8x12 slice. The times are simulated.
768 devices in a mesh: blk: 16 (over x, y_hi, core), dp: 48 (over z, y_lo).
Axes of the slice: x: 4, y: 8 (y_hi: 2, y_lo: 4; y = y_hi * 4 + y_lo), z: 12, core: 2. Of those that a mesh axis runs over, the one named last changes fastest.
Arguments:
- acts: bfloat16 [98304, 4096], P(('blk', 'dp')), may hold values from -6 to 6
- cotangent: bfloat16 [98304, 512], P(('blk', 'dp')), may hold values from -6 to 6
- kv_weight: bfloat16 [4096, 512], P('blk'), may hold values from -0.09375 to 0.09375
- batch_counts: int32 [768], P(('blk', 'dp')), may hold values from 1 to 4, as said below
Outputs:
- projected: bfloat16 [98304, 512], P(('blk', 'dp'))
- act_grad: bfloat16 [98304, 4096], P(('blk', 'dp'))
- weight_grad: float32 [4096, 512], P('blk')
Inputs may be any that keep to these rules, and one draw needn't show every extreme that they name: `batch_counts`: some worker has all 4 micro-batches live and some worker only one.
All inputs are finite; a program needn't handle non-finite values.
Results may differ from a plain program's by a relative error of at most 0.001.
Values may be sent and summed in bfloat16 or wider, within the bound.
No kernel may reach another device: no remote copies, remote signals or barrier semaphores. Data moves between devices by JAX's collectives and lax.ppermute only.
A program may use at most 32 MiB of HBM per device.

v0:
```python
import jax
import jax.numpy as jnp
from jax import lax
from jax.sharding import PartitionSpec as P

MICRO = 32


def per_device(acts, cotangent, kv_weight, batch_counts):
    tok_rows = acts.shape[0]
    shard_rows = kv_weight.shape[0]
    out_width = kv_weight.shape[1]
    loop_size = lax.axis_size("blk")
    live = (jnp.arange(tok_rows, dtype=jnp.int32) < batch_counts[0] * MICRO)[:, None]
    masked = jnp.where(live, cotangent, jnp.zeros_like(cotangent))
    full_weight = lax.all_gather(kv_weight, "blk", axis=0, tiled=True)
    product = jnp.dot(acts, full_weight, preferred_element_type=jnp.float32)
    act_total = jnp.dot(masked, full_weight.T, preferred_element_type=jnp.float32)
    projected = jnp.where(live, product, 0.0).astype(jnp.bfloat16)
    act_grad = act_total.astype(jnp.bfloat16)
    features = lax.all_to_all(acts, "blk", split_axis=1, concat_axis=0, tiled=True)
    gathered = lax.all_gather(masked, "blk", axis=0, tiled=True)
    features = features.reshape(loop_size, tok_rows, shard_rows)
    gathered = gathered.reshape(loop_size, tok_rows, out_width)
    summed = jnp.einsum("stc,sth->ch", features, gathered, preferred_element_type=jnp.float32)
    total = lax.psum(summed, "dp")
    all_tokens = tok_rows * loop_size * lax.axis_size("dp")
    weight_grad = total * float(all_tokens) ** (-0.5)
    return (projected, act_grad, weight_grad)


def solution(mesh):
    return jax.shard_map(
        per_device,
        mesh=mesh,
        in_specs=(P(("blk", "dp"), None), P(("blk", "dp"), None), P("blk", None), P(("blk", "dp"))),
        out_specs=(P(("blk", "dp"), None), P(("blk", "dp"), None), P("blk", None)),
        check_vma=False,
    )
```

profile of v0, /device:TPU:1, one launch (start us, length us, event | category | flops | bytes accessed | tf_op | source)
XLA Modules:
  0.0 642.0 jit_solution(18047297372189559239)
XLA Ops:
  7.2 0.0 all-gather.5.cloned.1.call-start
  7.9 1.6 broadcast_select_fusion
  9.5 0.0 all-gather.5.cloned.1.call-update
  9.5 0.0 all-reduce.2.cloned.1.call-start
  9.6 1.6 copy.9
  11.2 0.5 copy.10
  11.8 0.0 copy-start.1
  11.8 43.1 %all_to_all.16 = bf16[128,16,256]{2,0,1:T(8,128)(2,1)S(1)} all-to-all(bf16[128,16,256]{2,0,1:T(8,128)(2,1)S(1)} %copy.10), channel_id=1, replica_groups=mesh['blk'=16,'dp'=48] {'blk'}, dimensions={1} | all-to-all | bytes 2097152 | tf_op jit(solution)/shard_map/all_to_all | solution.py:21
  54.8 45.0 %all-gather.5.cloned.1.call-done = bf16[2048,512]{1,0:T(8,128)(2,1)} async-done(((bf16[128,512]{1,0:T(8,128)(2,1)}), bf16[2048,512]{1,0:T(8,128)(2,1)}) %all-gather.5.cloned.1.call-update) | async-done | bytes 2097168 | tf_op jit(solution)/shard_map/all_gather | solution.py:22
  99.8 3.1 convolution_bitcast_fusion
  102.9 0.0 copy-start.2
  102.9 0.0 all-reduce.2.cloned.1.call-update
  103.0 0.0 all-gather.3.cloned.1.call-start
  103.0 0.7 all-gather.3.cloned.1.call-update
  103.7 402.0 %all-reduce.2.cloned.1.call-done = f32[256,512]{0,1:T(8,128)} async-done(((f32[256,512]{0,1:T(8,128)}), f32[256,512]{0,1:T(8,128)}) %all-reduce.2.cloned.1.call-update) | async-done | bytes 524304 | tf_op jit(solution)/shard_map/psum | solution.py:26
  505.7 1.1 broadcast_multiply_fusion
  506.8 1.0 copy.12
  507.8 121.5 %all-gather.3.cloned.1.call-done = bf16[4096,512]{1,0:T(8,128)(2,1)} async-done(((bf16[256,512]{1,0:T(8,128)(2,1)}), bf16[4096,512]{1,0:T(8,128)(2,1)}) %all-gather.3.cloned.1.call-update) | async-done | bytes 4194320 | tf_op jit(solution)/shard_map/all_gather | solution.py:16
  629.3 0.0 copy-done.1
  629.3 0.0 copy-start
  629.3 3.7 fusion
  633.0 0.0 copy-done.2
  633.0 0.0 copy-done
  633.0 2.4 convolution_convert_fusion
  (1 shorter events, 0.0 us)
Async XLA Ops:
  7.2 92.7 %all-gather.5.cloned.1.call-start = ((), (), s32[]{:S(2)}) async-start(), calls=%async_computation.2 | async-start | bytes 2228224 | tf_op jit(solution)/shard_map/all_gather | solution.py:22
  9.5 496.2 %all-reduce.2.cloned.1.call-start = ((), (), s32[]{:S(2)}) async-start(), calls=%async_computation.3 | async-start | bytes 1048576 | tf_op jit(solution)/shard_map/psum | solution.py:26
  11.8 617.5 %copy-start.1 = (bf16[128,4096]{1,0:T(8,128)(2,1)S(1)}, bf16[128,4096]{1,0:T(8,128)(2,1)}, u32[]{:S(2)}) copy-start(bf16[128,4096]{1,0:T(8,128)(2,1)} %param.4) | copy-start | bytes 3145732
  102.9 530.1 %copy-start.2 = (bf16[128,512]{1,0:T(8,128)(2,1)S(1)}, bf16[128,512]{1,0:T(8,128)(2,1)}, u32[]{:S(2)}) copy-start(bf16[128,512]{1,0:T(8,128)(2,1)} %broadcast_select_fusion) | copy-start | bytes 393220
  103.0 526.3 %all-gather.3.cloned.1.call-start = ((), (), s32[]{:S(2)}) async-start(), calls=%async_computation.1 | async-start | bytes 4456448 | tf_op jit(solution)/shard_map/all_gather | solution.py:16
  629.3 3.7 copy-start
Sparse Core Ops, SparseCore 0:
  12.4 87.3 all-gather.4
  103.6 402.0 all-reduce.1
  510.2 119.0 all-gather.2
where the time goes:
time: 642 us
  waiting for transfers between devices  569 us (89%)
  blocking collectives  43.1 us (7%)
  between operations  14.4 us (2%)
  matrix products  9.29 us (1%)
    psum x1, waiting for transfers between devices, per_device(): total = lax.psum(summed, 'dp')  402 us
    all_gather x1, waiting for transfers between devices, per_device(): full_weight = lax.all_gather(kv_weight, 'blk', axis=0, tiled=True)  122 us
    all_gather x1, waiting for transfers between devices, per_device(): gathered = lax.all_gather(masked, 'blk', axis=0, tiled=True)  45 us
    all_to_all x1, blocking collectives, per_device(): lax.all_to_all(acts, 'blk', split_axis=1, concat_axis=0, tiled=True)  43.1 us
  transfers between devices with their start and end apart: 3, of which 3 were waited for; matrix products, arithmetic and copies ran while one was open for 1% of the time, Pallas kernels for 0%

commit v1 on v0

v1 whole, which is shorter than its diff:
```python
import functools

import jax
import jax.numpy as jnp
from jax import lax
from jax.experimental import pallas as pl
from jax.experimental.pallas import tpu as pltpu
from jax.sharding import Mesh, PartitionSpec as P

MICRO = 32
X, YH, CORE, ZH, ZL, YL = 4, 2, 2, 3, 4, 4
SIZES = (X, YH, CORE, ZH, ZL, YL)
NAMES = ("x", "yh", "core", "zh", "zl", "yl")
TOK, DIN, HD = 128, 4096, 512
SHARD = DIN // (X * YH * CORE)
PEERS = X * CORE
PIECES = YH * ZL * YL
ROWS = SHARD // (ZL * YL)
SCALE = float(TOK * X * YH * CORE * ZH * ZL * YL) ** -0.5

VMEM = pl.BlockSpec(memory_space=pltpu.VMEM)
SMEM = pl.BlockSpec(memory_space=pltpu.SMEM)
PARAMS = pltpu.CompilerParams(vmem_limit_bytes=40 * 1024 * 1024)


def pack_kernel(counts, acts, cot, out, masked):
    rows = lax.broadcasted_iota(jnp.int32, (TOK, HD), 0)
    kept = jnp.where(rows < counts[0] * MICRO, cot[...].astype(jnp.float32), 0.0)
    kept = kept.astype(jnp.bfloat16)
    masked[...] = kept
    for x in range(X):
        for c in range(CORE):
            peer = x * CORE + c
            for yh in range(YH):
                b = (x * YH + yh) * CORE + c
                out[peer, 0:TOK, yh * SHARD:(yh + 1) * SHARD] = acts[:, b * SHARD:(b + 1) * SHARD]
            out[peer, TOK:2 * TOK, :] = kept


def grad_kernel(place, got, own, near, far, out, pair):
    cols = 128
    right = got[:, TOK:2 * TOK, :].reshape(PEERS * TOK, HD)
    for i in range(YH * SHARD // cols):
        left = got[:, 0:TOK, i * cols:(i + 1) * cols].reshape(PEERS * TOK, cols)
        part = lax.dot_general(left, right, (((0,), (0,)), ((), ())), preferred_element_type=jnp.float32)
        out[i * (cols // ROWS):(i + 1) * (cols // ROWS)] = part.reshape(cols // ROWS, ROWS, HD)
    yh, yl = place[0], place[1]
    pair[yh] = own[...]

    @pl.when((yl == 0) | (yl == YL - 1))
    def _():
        pair[1 - yh] = near[...]

    @pl.when((yl != 0) & (yl != YL - 1))
    def _():
        pair[1 - yh] = far[...]


def project_kernel(place, counts, acts, masked, w0, w1, w2, w3, other, projected, act_grad):
    x, c = place[0], place[1]
    total = jnp.zeros((TOK, HD), jnp.float32)
    mk = masked[...]
    mine = (w0, w1, w2, w3)
    for k in range(X):
        xs = lax.rem(x - k + X, X)
        for side in range(CORE):
            cs = c if side == 0 else 1 - c
            for yh in range(YH):
                w = mine[k][yh] if side == 0 else other[k, yh]
                start = pl.multiple_of(((xs * YH + yh) * CORE + cs) * SHARD, SHARD)
                total += jnp.dot(acts[:, pl.ds(start, SHARD)], w, preferred_element_type=jnp.float32)
                back = lax.dot_general(mk, w, (((1,), (1,)), ((), ())), preferred_element_type=jnp.float32)
                act_grad[:, pl.ds(start, SHARD)] = back.astype(jnp.bfloat16)
    rows = lax.broadcasted_iota(jnp.int32, (TOK, HD), 0)
    projected[...] = jnp.where(rows < counts[0] * MICRO, total, 0.0).astype(jnp.bfloat16)


def sds(shape, dtype):
    return jax.ShapeDtypeStruct(shape, dtype)


def y_permute(value, pairs):
    return lax.ppermute(value, ("yh", "yl"), pairs)


def spread(piece, axes, count):
    return lax.all_to_all(jnp.broadcast_to(piece[None], (count,) + piece.shape), axes, 0, 0, tiled=True)


def per_device(acts, cotangent, kv_weight, batch_counts):
    x, c = lax.axis_index("x"), lax.axis_index("core")
    yh, yl = lax.axis_index("yh"), lax.axis_index("yl")
    bf16, f32 = jnp.bfloat16, jnp.float32

    near = y_permute(kv_weight, [(4, 3), (7, 0), (3, 4), (0, 7)])
    far = y_permute(kv_weight, [(4, 2), (7, 1), (3, 5), (0, 6)])

    packed, masked = pl.pallas_call(
        pack_kernel,
        out_shape=(sds((PEERS, 2 * TOK, HD), bf16), sds((TOK, HD), bf16)),
        in_specs=[SMEM, VMEM, VMEM],
        out_specs=(VMEM, VMEM),
        compiler_params=PARAMS,
        name="pack",
    )(batch_counts, acts, cotangent)
    got = lax.all_to_all(packed, ("x", "core"), 0, 0, tiled=True)

    partial, pair = pl.pallas_call(
        grad_kernel,
        out_shape=(sds((PIECES, ROWS, HD), f32), sds((YH, SHARD, HD), bf16)),
        in_specs=[SMEM, VMEM, VMEM, VMEM, VMEM],
        out_specs=(VMEM, VMEM),
        compiler_params=PARAMS,
        name="grad",
    )(jnp.stack([yh, yl]), got, kv_weight, near, far)

    parts = lax.all_to_all(partial, ("yh", "zl", "yl"), 0, 0, tiled=True)

    turned = [lax.ppermute(pair, "x", [(i, (i + k) % X) for i in range(X)]) for k in range(1, X)]
    line = jnp.stack([pair] + turned)
    other = lax.ppermute(line, "core", [(0, 1), (1, 0)])

    piece = jnp.sum(parts, axis=0) * SCALE
    piece = jnp.sum(spread(piece, "zh", ZH), axis=0)
    weight_grad = spread(piece, ("zl", "yl"), ZL * YL).reshape(SHARD, HD)

    projected, act_grad = pl.pallas_call(
        project_kernel,
        out_shape=(sds((TOK, HD), bf16), sds((TOK, DIN), bf16)),
        in_specs=[SMEM, SMEM] + [VMEM] * 7,
        out_specs=(VMEM, VMEM),
        compiler_params=PARAMS,
        name="project",
    )(jnp.stack([x, c]), batch_counts, acts, masked, pair, *turned, other)
    return projected, act_grad, weight_grad


def solution(mesh):
    inner = Mesh(mesh.devices.reshape(SIZES), NAMES)
    return jax.shard_map(
        per_device,
        mesh=inner,
        in_specs=(P(NAMES, None), P(NAMES, None), P(("x", "yh", "core"), None), P(NAMES)),
        out_specs=(P(NAMES, None), P(NAMES, None), P(("x", "yh", "core"), None)),
        check_vma=False,
    )
```

time: 642 us -> 134 us (0.21)
  waiting for transfers between devices: 569 us -> 52.2 us
  starting transfers between devices: 0.12 us -> 41.9 us
  blocking collectives: 43.1 us -> 17.7 us
  between operations: 14.4 us -> 1.45 us
  matrix products: 9.29 us -> 0 us
  local copies, waits for them, and re-layouts: 3.16 us -> 11.3 us
    psum x1 -> x0, waiting for transfers between devices: 402 us -> none  [per_device(): total = lax.psum(summed, 'dp')]
    all_gather x2 -> x0, waiting for transfers between devices: 166 us -> none  [the longest x1 122 us: per_device(): full_weight = lax.all_gather(kv_weight, 'blk', axis=0, tiled=True)]
    ppermute x0 -> x6, waiting for transfers between devices: none -> 33.4 us  [the longest x3 23.4 us: per_device(): lax.ppermute(pair, 'x', [(i, (i + k) % X) for i in range(X)])]
    all_to_all x0 -> x3, starting transfers between devices: none -> 28.4 us  [the longest x1 14.2 us: per_device(): got = lax.all_to_all(packed, ('x', 'core'), 0, 0, tiled=True)]
    all_to_all x1, blocking collectives: 43.1 us -> 17.7 us  [spread(): lax.all_to_all(jnp.broadcast_to(piece[None], (count,) + piece.shape), axe...]
    all_to_all x0 -> x3, waiting for transfers between devices: none -> 18.7 us  [the longest x1 13 us: per_device(): got = lax.all_to_all(packed, ('x', 'core'), 0, 0, tiled=True)]
    ppermute x0 -> x6, starting transfers between devices: none -> 13.6 us  [the longest x3 7.83 us: per_device(): lax.ppermute(pair, 'x', [(i, (i + k) % X) for i in range(X)])]
    dot_general x3 -> x0, matrix products: 9.29 us -> none  [the longest x1 3.72 us: per_device(): product = jnp.dot(acts, full_weight, preferred_element_type=jnp.float32)]
  transfers between devices with their start and end apart: 3 -> 9, of which waited for: 3 -> 7; matrix products, arithmetic and copies ran while one was open for 1% -> 3% of each run, Pallas kernels for 0% -> 3%
where the time goes in v1:
time: 134 us; the launch traced here: 133 us
  waiting for transfers between devices  52.2 us (39%)
  starting transfers between devices  41.9 us (31%)
  blocking collectives  17.7 us (13%)
  local copies, waits for them, and re-layouts  11.3 us (8%)
  Pallas kernels  4.95 us (4%)
  other arithmetic  3.05 us (2%)
  between operations  1.45 us (1%)
    ppermute x3, waiting for transfers between devices, per_device(): lax.ppermute(pair, 'x', [(i, (i + k) % X) for i in range(X)])  23.4 us
    all_to_all x1, blocking collectives, spread(): lax.all_to_all(jnp.broadcast_to(piece[None], (count,) + piece.shape), axe...  17.7 us
    all_to_all x1, starting transfers between devices, per_device(): got = lax.all_to_all(packed, ('x', 'core'), 0, 0, tiled=True)  14.2 us
    all_to_all x1, waiting for transfers between devices, per_device(): got = lax.all_to_all(packed, ('x', 'core'), 0, 0, tiled=True)  13 us
    unnamed x29, local copies, waits for them, and re-layouts  10.5 us
    ppermute x2, waiting for transfers between devices, y_permute(): return lax.ppermute(value, ('yh', 'yl'), pairs)  10 us
    all_to_all x1, starting transfers between devices, spread(): lax.all_to_all(jnp.broadcast_to(piece[None], (count,) + piece.shape), axe...  9.56 us
    ppermute x3, starting transfers between devices, per_device(): lax.ppermute(pair, 'x', [(i, (i + k) % X) for i in range(X)])  7.83 us
  transfers between devices with their start and end apart: 9, of which 7 were waited for; matrix products, arithmetic and copies ran while one was open for 3% of the time, Pallas kernels for 3%

profile of v1, /device:TPU:1, one launch (start us, length us, event | category | flops | bytes accessed | tf_op | source)
XLA Modules:
  0.0 132.6 jit_solution(830562078428540235)
XLA Ops:
  1.3 1.2 copy-done
  3.6 1.3 copy-done.2
  4.9 14.2 %all-to-all-start = ((bf16[8,256,512]{2,1,0:T(8,128)(2,1)}), bf16[8,256,512]{2,1,0:T(8,128)(2,1)S(1)}, u32[]{:S(2)}, u32[]{:S(2)}) async-start(bf16[8,256,512]{2,1,0:T(8,128)(2,1)} %copy-done.2), calls=%async_computation | async-start | bytes 4194304 | tf_op jit(solution)/shard_map/all_to_all | solution.py:106
  19.1 1.9 %collective-permute-start = (bf16[256,512]{1,0:T(8,128)(2,1)S(1)}, bf16[256,512]{1,0:T(8,128)(2,1)S(1)}, u32[]{:S(2)}, u32[]{:S(2)}) collective-permute-start(bf16[256,512]{1,0:T(8,128)(2,1)S(1)} %copy-done.12), channel_id=1, source_target_pairs={{96,3},{99,0},{3,96},{0,99},{100,7},{103,4},{7,100},{4,103},{104,1... | collective-permute-start | bytes 786440 | tf_op jit(solution)/shard_map/ppermute | solution.py:83
  21.0 1.3 collective-permute-start.1
  22.4 7.6 %collective-permute-done.near = bf16[256,512]{1,0:T(8,128)(2,1)S(1)} collective-permute-done((bf16[256,512]{1,0:T(8,128)(2,1)S(1)}, bf16[256,512]{1,0:T(8,128)(2,1)S(1)}, u32[]{:S(2)}, u32[]{:S(2)}) %collective-permute-start) | collective-permute-done | bytes 262176 | tf_op jit(solution)/shard_map/ppermute | solution.py:83
  29.9 2.5 %collective-permute-done.1.far = bf16[256,512]{1,0:T(8,128)(2,1)S(1)} collective-permute-done((bf16[256,512]{1,0:T(8,128)(2,1)S(1)}, bf16[256,512]{1,0:T(8,128)(2,1)S(1)}, u32[]{:S(2)}, u32[]{:S(2)}) %collective-permute-start.1) | collective-permute-done | bytes 262176 | tf_op jit(solution)/shard_map/ppermute | solution.py:83
  32.4 13.0 %all-to-all-done.got = bf16[8,256,512]{2,1,0:T(8,128)(2,1)S(1)} async-done(((bf16[8,256,512]{2,1,0:T(8,128)(2,1)}), bf16[8,256,512]{2,1,0:T(8,128)(2,1)S(1)}, u32[]{:S(2)}, u32[]{:S(2)}) %all-to-all-start) | async-done | bytes 2097184 | tf_op jit(solution)/shard_map/all_to_all | solution.py:106
  45.4 1.3 grad.1
  47.7 4.7 %all-to-all-start.1 = ((f32[32,16,512]{2,1,0:T(8,128)}), f32[32,16,512]{2,1,0:T(8,128)}, u32[]{:S(2)}, u32[]{:S(2)}) async-start(f32[32,16,512]{2,1,0:T(8,128)} %copy-done.11), calls=%async_computation.1 | async-start | bytes 2097152 | tf_op jit(solution)/shard_map/all_to_all | solution.py:117
  52.4 2.8 %collective-permute-start.4 = (bf16[2,256,512]{2,1,0:T(8,128)(2,1)S(1)}, bf16[2,256,512]{2,1,0:T(8,128)(2,1)S(1)}, u32[]{:S(2)}, u32[]{:S(2)}) collective-permute-start(bf16[2,256,512]{2,1,0:T(8,128)(2,1)S(1)} %get-tuple-element.11.w0), channel_id=1, source_target_pairs={{0,576},{192,0},{384,192},{576,384},{1,577},{193,1},{385,193},{577... | collective-permute-start | bytes 1572872 | tf_op jit(solution)/shard_map/ppermute | solution.py:119
  55.2 3.1 %collective-permute-start.3 = (bf16[2,256,512]{2,1,0:T(8,128)(2,1)S(1)}, bf16[2,256,512]{2,1,0:T(8,128)(2,1)S(1)}, u32[]{:S(2)}, u32[]{:S(2)}) collective-permute-start(bf16[2,256,512]{2,1,0:T(8,128)(2,1)S(1)} %get-tuple-element.11.w0), channel_id=1, source_target_pairs={{0,384},{192,576},{384,0},{576,192},{1,385},{193,577},{385,1},{577... | collective-permute-start | bytes 1572872 | tf_op jit(solution)/shard_map/ppermute | solution.py:119
  58.3 1.9 %collective-permute-start.2 = (bf16[2,256,512]{2,1,0:T(8,128)(2,1)S(1)}, bf16[2,256,512]{2,1,0:T(8,128)(2,1)S(1)}, u32[]{:S(2)}, u32[]{:S(2)}) collective-permute-start(bf16[2,256,512]{2,1,0:T(8,128)(2,1)S(1)} %get-tuple-element.11.w0), channel_id=1, source_target_pairs={{0,192},{192,384},{384,576},{576,0},{1,193},{193,385},{385,577},{5... | collective-permute-start | bytes 1572872 | tf_op jit(solution)/shard_map/ppermute | solution.py:119
  60.2 6.5 %collective-permute-done.4.w3 = bf16[2,256,512]{2,1,0:T(8,128)(2,1)S(1)} collective-permute-done((bf16[2,256,512]{2,1,0:T(8,128)(2,1)S(1)}, bf16[2,256,512]{2,1,0:T(8,128)(2,1)S(1)}, u32[]{:S(2)}, u32[]{:S(2)}) %collective-permute-start.4) | collective-permute-done | bytes 524320 | tf_op jit(solution)/shard_map/ppermute | solution.py:119
  66.8 4.0 %collective-permute-done.3.w2 = bf16[2,256,512]{2,1,0:T(8,128)(2,1)S(1)} collective-permute-done((bf16[2,256,512]{2,1,0:T(8,128)(2,1)S(1)}, bf16[2,256,512]{2,1,0:T(8,128)(2,1)S(1)}, u32[]{:S(2)}, u32[]{:S(2)}) %collective-permute-start.3) | collective-permute-done | bytes 524320 | tf_op jit(solution)/shard_map/ppermute | solution.py:119
  70.8 12.8 %collective-permute-done.2.w1 = bf16[2,256,512]{2,1,0:T(8,128)(2,1)S(1)} collective-permute-done((bf16[2,256,512]{2,1,0:T(8,128)(2,1)S(1)}, bf16[2,256,512]{2,1,0:T(8,128)(2,1)S(1)}, u32[]{:S(2)}, u32[]{:S(2)}) %collective-permute-start.2) | collective-permute-done | bytes 524320 | tf_op jit(solution)/shard_map/ppermute | solution.py:119
  83.6 1.6 %pad_maximum_fusion = bf16[4,2,256,512]{3,2,1,0:T(8,128)(2,1)} fusion(bf16[1,2,256,512]{3,2,1,0:T(8,128)(2,1)S(1)} %bitcast.10, bf16[1,2,256,512]{3,2,1,0:T(8,128)(2,1)S(1)} %bitcast.11, bf16[1,2,256,512]{3,2,1,0:T(8,128)(2,1)S(1)} %bitcast.12, bf16[1,2,256,512]{3,2,1,0:T(8,128)(2,1)S(1)} %bitcast.9), kind=kLoop, calls=%fused_computation | loop fusion | flops 3145728 | bytes 4194304 | tf_op jit(solution)/shard_map/stack | solution.py:120
  85.2 2.5 %collective-permute-start.5 = (bf16[4,2,256,512]{3,2,1,0:T(8,128)(2,1)}, bf16[4,2,256,512]{3,2,1,0:T(8,128)(2,1)S(1)}, u32[]{:S(2)}, u32[]{:S(2)}) collective-permute-start(bf16[4,2,256,512]{3,2,1,0:T(8,128)(2,1)} %pad_maximum_fusion), channel_id=1, source_target_pairs={{0,48},{48,0},{1,49},{49,1},{2,50},{50,2},{3,51},{51,3},{4,52},{52... | collective-permute-start | bytes 6291464 | tf_op jit(solution)/shard_map/ppermute | solution.py:121
  87.8 1.3 reduce_sum.18
  89.1 17.7 %all_to_all.20 = f32[3,16,512]{2,1,0:T(8,128)S(1)} all-to-all(f32[3,16,512]{2,1,0:T(8,128)S(1)} %broadcast_in_dim.4), channel_id=1, replica_groups=mesh['x'=4,'yh'=2,'core'=2,'zh'=3,'zl'=4,'yl'=4] {'zh'}, dimensions={0} | all-to-all | bytes 196608 | tf_op jit(solution)/shard_map/all_to_all | solution.py:87
  107.7 9.6 %all-to-all-start.3 = ((f32[16,16,512]{2,1,0:T(8,128)}), f32[16,16,512]{2,1,0:T(8,128)}, u32[]{:S(2)}, u32[]{:S(2)}) async-start(f32[16,16,512]{2,1,0:T(8,128)} %broadcast_in_dim.5), calls=%async_computation.3 | async-start | bytes 1048576 | tf_op jit(solution)/shard_map/all_to_all | solution.py:87
  121.5 3.5 %project.1 = (bf16[128,512]{1,0:T(8,128)(2,1)}, bf16[128,4096]{1,0:T(8,128)(2,1)}) custom-call(s32[2]{0:T(128)S(1)} %pad_add_fusion.place, s32[1]{0:T(128)S(6)} %copy.8.counts, bf16[128,4096]{1,0:T(8,128)(2,1)S(1)} %copy-done.1, bf16[128,512]{1,0:T(8,128)(2,1)S(1)} %get-tuple-element.9.masked, bf16[2,256,512]{2,1,0:T(8,128)(2,1)S(1)} %copy-done.4, ...), custom_call_target="tpu_custom_call" | custom-call | tf_op jit(solution)/shard_map/project/pallas_call | solution.py:127
  125.0 5.7 %all-to-all-done.3 = f32[16,16,512]{2,1,0:T(8,128)} async-done(((f32[16,16,512]{2,1,0:T(8,128)}), f32[16,16,512]{2,1,0:T(8,128)}, u32[]{:S(2)}, u32[]{:S(2)}) %all-to-all-start.3) | async-done | bytes 524320 | tf_op jit(solution)/shard_map/all_to_all | solution.py:87
  130.7 1.9 %copy.9 = f32[256,512]{1,0:T(8,128)} copy(f32[256,512]{1,0:T(8,128)} %bitcast.8) | data formatting | bytes 1048576
  (35 shorter events, 7.3 us)
Async XLA Ops:
  1.3 1.2 copy-start
  2.5 0.9 copy-start.13
  3.6 1.3 %copy-start.2 = (bf16[8,256,512]{2,1,0:T(8,128)(2,1)}, bf16[8,256,512]{2,1,0:T(8,128)(2,1)S(1)}, u32[]{:S(2)}) copy-start(bf16[8,256,512]{2,1,0:T(8,128)(2,1)S(1)} %get-tuple-element.10) | copy-start | bytes 6291460
  4.9 14.2 %copy-start.12 = (bf16[256,512]{1,0:T(8,128)(2,1)S(1)}, bf16[256,512]{1,0:T(8,128)(2,1)}, u32[]{:S(2)}) copy-start(bf16[256,512]{1,0:T(8,128)(2,1)} %own.1) | copy-start | bytes 786436
  4.9 40.5 %all-to-all-start = ((bf16[8,256,512]{2,1,0:T(8,128)(2,1)}), bf16[8,256,512]{2,1,0:T(8,128)(2,1)S(1)}, u32[]{:S(2)}, u32[]{:S(2)}) async-start(bf16[8,256,512]{2,1,0:T(8,128)(2,1)} %copy-done.2), calls=%async_computation | async-start | bytes 4194304 | tf_op jit(solution)/shard_map/all_to_all | solution.py:106
  19.1 10.9 %collective-permute-start = (bf16[256,512]{1,0:T(8,128)(2,1)S(1)}, bf16[256,512]{1,0:T(8,128)(2,1)S(1)}, u32[]{:S(2)}, u32[]{:S(2)}) collective-permute-start(bf16[256,512]{1,0:T(8,128)(2,1)S(1)} %copy-done.12), channel_id=1, source_target_pairs={{96,3},{99,0},{3,96},{0,99},{100,7},{103,4},{7,100},{4,103},{104,1... | collective-permute-start | bytes 786440 | tf_op jit(solution)/shard_map/ppermute | solution.py:83
  21.0 11.4 %collective-permute-start.1 = (bf16[256,512]{1,0:T(8,128)(2,1)S(1)}, bf16[256,512]{1,0:T(8,128)(2,1)S(1)}, u32[]{:S(2)}, u32[]{:S(2)}) collective-permute-start(bf16[256,512]{1,0:T(8,128)(2,1)S(1)} %copy-done.12), channel_id=1, source_target_pairs={{96,2},{99,1},{3,97},{0,98},{100,6},{103,5},{7,101},{4,102},{104,1... | collective-permute-start | bytes 786440 | tf_op jit(solution)/shard_map/ppermute | solution.py:83
  46.7 1.0 copy-start.11
  47.7 35.9 %copy-start.3 = (bf16[2,256,512]{2,1,0:T(8,128)(2,1)}, bf16[2,256,512]{2,1,0:T(8,128)(2,1)S(1)}, u32[]{:S(2)}) copy-start(bf16[2,256,512]{2,1,0:T(8,128)(2,1)S(1)} %get-tuple-element.11.w0) | copy-start | bytes 1572868
  47.7 40.1 %all-to-all-start.1 = ((f32[32,16,512]{2,1,0:T(8,128)}), f32[32,16,512]{2,1,0:T(8,128)}, u32[]{:S(2)}, u32[]{:S(2)}) async-start(f32[32,16,512]{2,1,0:T(8,128)} %copy-done.11), calls=%async_computation.1 | async-start | bytes 2097152 | tf_op jit(solution)/shard_map/all_to_all | solution.py:117
  52.4 14.4 %collective-permute-start.4 = (bf16[2,256,512]{2,1,0:T(8,128)(2,1)S(1)}, bf16[2,256,512]{2,1,0:T(8,128)(2,1)S(1)}, u32[]{:S(2)}, u32[]{:S(2)}) collective-permute-start(bf16[2,256,512]{2,1,0:T(8,128)(2,1)S(1)} %get-tuple-element.11.w0), channel_id=1, source_target_pairs={{0,576},{192,0},{384,192},{576,384},{1,577},{193,1},{385,193},{577... | collective-permute-start | bytes 1572872 | tf_op jit(solution)/shard_map/ppermute | solution.py:119
  55.2 15.6 %collective-permute-start.3 = (bf16[2,256,512]{2,1,0:T(8,128)(2,1)S(1)}, bf16[2,256,512]{2,1,0:T(8,128)(2,1)S(1)}, u32[]{:S(2)}, u32[]{:S(2)}) collective-permute-start(bf16[2,256,512]{2,1,0:T(8,128)(2,1)S(1)} %get-tuple-element.11.w0), channel_id=1, source_target_pairs={{0,384},{192,576},{384,0},{576,192},{1,385},{193,577},{385,1},{577... | collective-permute-start | bytes 1572872 | tf_op jit(solution)/shard_map/ppermute | solution.py:119
  58.3 25.3 %collective-permute-start.2 = (bf16[2,256,512]{2,1,0:T(8,128)(2,1)S(1)}, bf16[2,256,512]{2,1,0:T(8,128)(2,1)S(1)}, u32[]{:S(2)}, u32[]{:S(2)}) collective-permute-start(bf16[2,256,512]{2,1,0:T(8,128)(2,1)S(1)} %get-tuple-element.11.w0), channel_id=1, source_target_pairs={{0,192},{192,384},{384,576},{576,0},{1,193},{193,385},{385,577},{5... | collective-permute-start | bytes 1572872 | tf_op jit(solution)/shard_map/ppermute | solution.py:119
  66.8 18.5 %copy-start.5 = (bf16[2,256,512]{2,1,0:T(8,128)(2,1)}, bf16[2,256,512]{2,1,0:T(8,128)(2,1)S(1)}, u32[]{:S(2)}) copy-start(bf16[2,256,512]{2,1,0:T(8,128)(2,1)S(1)} %collective-permute-done.4.w3) | copy-start | bytes 1572868
  70.8 14.4 %copy-start.7 = (bf16[2,256,512]{2,1,0:T(8,128)(2,1)}, bf16[2,256,512]{2,1,0:T(8,128)(2,1)S(1)}, u32[]{:S(2)}) copy-start(bf16[2,256,512]{2,1,0:T(8,128)(2,1)S(1)} %collective-permute-done.3.w2) | copy-start | bytes 1572868
  83.6 1.6 %copy-start.9 = (bf16[2,256,512]{2,1,0:T(8,128)(2,1)}, bf16[2,256,512]{2,1,0:T(8,128)(2,1)S(1)}, u32[]{:S(2)}) copy-start(bf16[2,256,512]{2,1,0:T(8,128)(2,1)S(1)} %collective-permute-done.2.w1) | copy-start | bytes 1572868
  85.2 32.1 %copy-start.1 = (bf16[128,4096]{1,0:T(8,128)(2,1)S(1)}, bf16[128,4096]{1,0:T(8,128)(2,1)}, u32[]{:S(2)}) copy-start(bf16[128,4096]{1,0:T(8,128)(2,1)} %acts.3) | copy-start | bytes 3145732
  85.2 32.1 %collective-permute-start.5 = (bf16[4,2,256,512]{3,2,1,0:T(8,128)(2,1)}, bf16[4,2,256,512]{3,2,1,0:T(8,128)(2,1)S(1)}, u32[]{:S(2)}, u32[]{:S(2)}) collective-permute-start(bf16[4,2,256,512]{3,2,1,0:T(8,128)(2,1)} %pad_maximum_fusion), channel_id=1, source_target_pairs={{0,48},{48,0},{1,49},{49,1},{2,50},{50,2},{3,51},{51,3},{4,52},{52... | collective-permute-start | bytes 6291464 | tf_op jit(solution)/shard_map/ppermute | solution.py:121
  107.7 23.0 %all-to-all-start.3 = ((f32[16,16,512]{2,1,0:T(8,128)}), f32[16,16,512]{2,1,0:T(8,128)}, u32[]{:S(2)}, u32[]{:S(2)}) async-start(f32[16,16,512]{2,1,0:T(8,128)} %broadcast_in_dim.5), calls=%async_computation.3 | async-start | bytes 1048576 | tf_op jit(solution)/shard_map/all_to_all | solution.py:87
  117.3 1.0 copy-start.4
  118.4 1.0 copy-start.6
  119.4 1.0 copy-start.8
  120.5 1.0 copy-start.10

commit v2 on v0

v2 whole, which is shorter than its diff:
```python
import jax
import jax.numpy as jnp
from jax import lax
from jax.experimental import pallas as pl
from jax.experimental.pallas import tpu as pltpu
from jax.sharding import Mesh, PartitionSpec as P

MICRO = 32
X, YH, CORE, ZH, ZL, YL = 4, 2, 2, 3, 4, 4
SIZES = (X, YH, CORE, ZH, ZL, YL)
NAMES = ("x", "yh", "core", "zh", "zl", "yl")
TOK, DIN, HD = 128, 4096, 512
SHARD = DIN // (X * YH * CORE)
PEERS = X * CORE
PIECES = YH * ZL * YL
ROWS = SHARD // (ZL * YL)
LANES = 128
FLAT = ROWS * HD // LANES
TALL = FLAT + 8
SCALE = float(TOK * X * YH * CORE * ZH * ZL * YL) ** -0.5
TOP = 13.0

VMEM = pl.BlockSpec(memory_space=pltpu.VMEM)
SMEM = pl.BlockSpec(memory_space=pltpu.SMEM)
ANY = pl.BlockSpec(memory_space=pl.ANY)
TINY, SMALL, LARGE = 8 * 1024 * 1024, 16 * 1024 * 1024, 60 * 1024 * 1024
bf16, f16, f32 = jnp.bfloat16, jnp.float16, jnp.float32


def pack_kernel(counts, acts, cot, packed, masked, raw, kept, full, built, sems):
    wide = DIN // X
    first = pltpu.make_async_copy(cot, raw, sems.at[0])
    first.start()
    loads = [
        pltpu.make_async_copy(
            acts.at[:, x * wide:(x + 1) * wide], full.at[:, x * wide:(x + 1) * wide], sems.at[1 + x])
        for x in range(X)
    ]
    for load in loads:
        load.start()
    first.wait()
    rows = lax.broadcasted_iota(jnp.int32, (TOK, HD), 0)
    kept[...] = jnp.where(rows < counts[0] * MICRO, raw[...].astype(f32), 0.0).astype(bf16)
    stores = [pltpu.make_async_copy(kept, masked, sems.at[1 + X])]
    stores[0].start()
    for x in range(X):
        loads[x].wait()
        for side in range(CORE):
            peer = x * CORE + side
            for yh in range(YH):
                b = (x * YH + yh) * CORE + side
                built[peer, 0:TOK, yh * SHARD:(yh + 1) * SHARD] = full[:, b * SHARD:(b + 1) * SHARD]
            built[peer, TOK:2 * TOK, :] = kept[...]
        pieces = slice(x * CORE, (x + 1) * CORE)
        stores.append(pltpu.make_async_copy(built.at[pieces], packed.at[pieces], sems.at[2 + X + x]))
        stores[-1].start()
    for store in stores:
        store.wait()


def exponent(values):
    top = jnp.max(jnp.max(jnp.abs(values), axis=1, keepdims=True), axis=0, keepdims=True)
    return TOP - jnp.floor(jnp.log2(jnp.maximum(top, 2.0 ** -100)))


def encode(out, i, rows, power):
    for j in range(HD // LANES):
        out[i, j * ROWS:(j + 1) * ROWS, :] = rows[:, j * LANES:(j + 1) * LANES]
    out[i, FLAT:TALL, :] = jnp.broadcast_to(power, (TALL - FLAT, LANES))


def decode(ref, i):
    return ref[i, 0:FLAT, :] * jnp.exp2(-ref[i, FLAT:FLAT + 1, :])


def grad_kernel(got, pair, out, same, acc):
    cols = 128
    right = got[:, TOK:2 * TOK, :].reshape(PEERS * TOK, HD)
    for i in range(YH * SHARD // cols):
        left = got[:, 0:TOK, i * cols:(i + 1) * cols].reshape(PEERS * TOK, cols)
        acc[i * cols:(i + 1) * cols, :] = lax.dot_general(
            left, right, (((0,), (0,)), ((), ())), preferred_element_type=f32)
    power = exponent(acc[...])
    factor = jnp.exp2(power)
    for i in range(PIECES):
        encode(out, i, acc[i * ROWS:(i + 1) * ROWS, :] * factor, power)


def sum_kernel(parts, out):
    total = decode(parts, 0)
    for i in range(1, PIECES):
        total += decode(parts, i)
    for i in range(ZH):
        out[i] = total


def final_kernel(parts, out):
    total = parts[0]
    for i in range(1, ZH):
        total += parts[i]
    total = total * SCALE
    power = exponent(total)
    total = total * jnp.exp2(power)
    for i in range(ZL * YL):
        out[i, 0:FLAT, :] = total
        out[i, FLAT:TALL, :] = jnp.broadcast_to(power, (TALL - FLAT, LANES))


def unpack_kernel(got, out):
    for i in range(ZL * YL):
        value = decode(got, i)
        for j in range(HD // LANES):
            out[i * ROWS:(i + 1) * ROWS, j * LANES:(j + 1) * LANES] = value[j * ROWS:(j + 1) * ROWS, :]


def project_kernel(place, counts, acts, masked, after, w0, w1, w2, w3, projected, act_grad):
    x = place[0]
    kept = masked[...]
    total = jnp.zeros((TOK, HD), f32)
    for k, shards in enumerate((w0, w1, w2, w3)):
        group = lax.rem(x - k + X, X) * YH * CORE
        for core in range(CORE):
            for yh in range(YH):
                w = shards[core, yh]
                start = pl.multiple_of((group + yh * CORE + core) * SHARD, SHARD)
                total += jnp.dot(acts[:, pl.ds(start, SHARD)], w, preferred_element_type=f32)
                back = lax.dot_general(kept, w, (((1,), (1,)), ((), ())), preferred_element_type=f32)
                act_grad[:, pl.ds(start, SHARD)] = back.astype(bf16)
    rows = lax.broadcasted_iota(jnp.int32, (TOK, HD), 0)
    projected[...] = jnp.where(rows < counts[0] * MICRO, total, 0.0).astype(bf16)


def sds(shape, dtype):
    return jax.ShapeDtypeStruct(shape, dtype)


def call(body, outs, ins, out_specs, scratch=(), name=None, limit=SMALL, **more):
    return pl.pallas_call(
        body, out_shape=outs, in_specs=ins, out_specs=out_specs, scratch_shapes=list(scratch),
        compiler_params=pltpu.CompilerParams(vmem_limit_bytes=limit), name=name, **more)


def exchange(value, axes):
    return lax.all_to_all(value, axes, 0, 0, tiled=True)


def per_device(acts, cotangent, kv_weight, batch_counts):
    x, core = lax.axis_index("x"), lax.axis_index("core")
    yh, yl = lax.axis_index("yh"), lax.axis_index("yl")
    dma = pltpu.SemaphoreType.DMA

    packed, masked = call(
        pack_kernel, (sds((PEERS, 2 * TOK, HD), bf16), sds((TOK, HD), bf16)),
        [SMEM, ANY, ANY], (ANY, ANY),
        (pltpu.VMEM((TOK, HD), bf16), pltpu.VMEM((TOK, HD), bf16), pltpu.VMEM((TOK, DIN), bf16),
         pltpu.VMEM((PEERS, 2 * TOK, HD), bf16), dma((2 + 2 * X,))),
        "pack", LARGE,
    )(batch_counts, acts, cotangent)
    got = exchange(packed, ("x", "core"))

    near = lax.ppermute(kv_weight, ("yh", "yl"), [(4, 3), (7, 0), (3, 4), (0, 7)])
    far = lax.ppermute(kv_weight, ("yh", "yl"), [(4, 2), (7, 1), (3, 5), (0, 6)])
    twin = jnp.where((yl == 0) | (yl == YL - 1), near, far)
    pair = jnp.where(yh == 0, jnp.stack([kv_weight, twin]), jnp.stack([twin, kv_weight]))
    side = lax.ppermute(pair, "core", [(0, 1), (1, 0)])
    quad = jnp.where(core == 0, jnp.stack([pair, side]), jnp.stack([side, pair]))

    partial, quad = call(
        grad_kernel, (sds((PIECES, TALL, LANES), f32), sds((CORE, YH, SHARD, HD), bf16)),
        [VMEM, ANY], (VMEM, ANY), (pltpu.VMEM((YH * SHARD, HD), f32),), "grad",
        input_output_aliases={1: 1},
    )(got, quad)
    parts = exchange(partial.astype(f16), ("yh", "zl", "yl"))
    turned = [lax.ppermute(quad, "x", [(i, (i + k) % X) for i in range(X)]) for k in range(1, X)]
    piece = call(sum_kernel, sds((ZH, FLAT, LANES), f32), [VMEM], VMEM, name="sum", limit=TINY)(parts.astype(f32))
    pieces = exchange(piece, "zh")
    ready = call(
        final_kernel, sds((ZL * YL, TALL, LANES), f32), [VMEM], VMEM, name="final", limit=TINY)(pieces)
    whole = exchange(ready.astype(f16), ("zl", "yl"))

    projected, act_grad = call(
        project_kernel, (sds((TOK, HD), bf16), sds((TOK, DIN), bf16)),
        [SMEM, SMEM, VMEM, VMEM, ANY] + [VMEM] * 4, (VMEM, VMEM), (), "project", SMALL,
        cost_estimate=pl.CostEstimate(
            flops=4 * TOK * DIN * HD, bytes_accessed=2 * (2 * TOK * DIN + DIN * HD), transcendentals=0),
    )(x.reshape(1), batch_counts, acts, masked, ready, quad, *turned)

    weight_grad = call(
        unpack_kernel, sds((SHARD, HD), f32), [VMEM], VMEM, name="unpack", limit=TINY)(whole.astype(f32))
    return projected, act_grad, weight_grad


def solution(mesh):
    inner = Mesh(mesh.devices.reshape(SIZES), NAMES)
    return jax.shard_map(
        per_device,
        mesh=inner,
        in_specs=(P(NAMES, None), P(NAMES, None), P(("x", "yh", "core"), None), P(NAMES)),
        out_specs=(P(NAMES, None), P(NAMES, None), P(("x", "yh", "core"), None)),
        check_vma=False,
    )
```

time: 642 us -> 109 us (0.17)
  waiting for transfers between devices: 569 us -> 38 us
  starting transfers between devices: 0.12 us -> 36.8 us
  blocking collectives: 43.1 us -> 17.9 us
  between operations: 14.4 us -> 1.46 us
  matrix products: 9.29 us -> 0 us
  Pallas kernels: 0 us -> 9.28 us
    psum x1 -> x0, waiting for transfers between devices: 402 us -> none  [per_device(): total = lax.psum(summed, 'dp')]
    all_gather x2 -> x0, waiting for transfers between devices: 166 us -> none  [the longest x1 122 us: per_device(): full_weight = lax.all_gather(kv_weight, 'blk', axis=0, tiled=True)]
    all_to_all x1, blocking collectives: 43.1 us -> 17.9 us  [exchange(): return lax.all_to_all(value, axes, 0, 0, tiled=True)]
    all_to_all x0 -> x3, starting transfers between devices: none -> 22.4 us  [exchange(): return lax.all_to_all(value, axes, 0, 0, tiled=True)]
    ppermute x0 -> x6, waiting for transfers between devices: none -> 21 us  [the longest x3 9.33 us: per_device(): lax.ppermute(quad, 'x', [(i, (i + k) % X) for i in range(X)])]
    all_to_all x0 -> x3, waiting for transfers between devices: none -> 16.9 us  [exchange(): return lax.all_to_all(value, axes, 0, 0, tiled=True)]
    ppermute x0 -> x6, starting transfers between devices: none -> 14.3 us  [the longest x3 8.54 us: per_device(): lax.ppermute(quad, 'x', [(i, (i + k) % X) for i in range(X)])]
    dot_general x3 -> x0, matrix products: 9.29 us -> none  [the longest x1 3.72 us: per_device(): product = jnp.dot(acts, full_weight, preferred_element_type=jnp.float32)]
  transfers between devices with their start and end apart: 3 -> 9, of which waited for: 3 -> 7; matrix products, arithmetic and copies ran while one was open for 1% -> 3% of each run, Pallas kernels for 0% -> 5%
where the time goes in v2:
time: 109 us; the launch traced here: 108 us
  waiting for transfers between devices  38 us (35%)
  starting transfers between devices  36.8 us (34%)
  blocking collectives  17.9 us (16%)
  Pallas kernels  9.28 us (9%)
  other arithmetic  4.15 us (4%)
  between operations  1.46 us (1%)
    all_to_all x3, starting transfers between devices, exchange(): return lax.all_to_all(value, axes, 0, 0, tiled=True)  22.4 us
    all_to_all x1, blocking collectives, exchange(): return lax.all_to_all(value, axes, 0, 0, tiled=True)  17.9 us
    all_to_all x3, waiting for transfers between devices, exchange(): return lax.all_to_all(value, axes, 0, 0, tiled=True)  16.9 us
    ppermute x3, waiting for transfers between devices, per_device(): lax.ppermute(quad, 'x', [(i, (i + k) % X) for i in range(X)])  9.33 us
    ppermute x3, starting transfers between devices, per_device(): lax.ppermute(quad, 'x', [(i, (i + k) % X) for i in range(X)])  8.54 us
    ppermute x1, waiting for transfers between devices, per_device(): lax.ppermute(kv_weight, ('yh', 'yl'), [(4, 3), (7, 0), (3, 4), (0, 7)])  7.62 us
    pallas_call x1, Pallas kernels, per_device(): call(project_kernel, (sds((TOK, HD), bf16), sds((TOK, DIN), bf16)), [SMEM...  4.8 us
    ppermute x1, starting transfers between devices, per_device(): side = lax.ppermute(pair, 'core', [(0, 1), (1, 0)])  2.6 us
  transfers between devices with their start and end apart: 9, of which 7 were waited for; matrix products, arithmetic and copies ran while one was open for 3% of the time, Pallas kernels for 5%

profile of v2, /device:TPU:1, one launch (start us, length us, event | category | flops | bytes accessed | tf_op | source)
XLA Modules:
  0.0 108.3 jit_solution(3736608943401703748)
XLA Ops:
  1.3 2.5 %pack.1 = (bf16[8,256,512]{2,1,0:T(8,128)(2,1)}, bf16[128,512]{1,0:T(8,128)(2,1)}) custom-call(s32[1]{0:T(128)S(6)} %copy.9.counts, bf16[128,4096]{1,0:T(8,128)(2,1)} %acts.3, bf16[128,512]{1,0:T(8,128)(2,1)} %cot.1), custom_call_target="tpu_custom_call" | custom-call | tf_op jit(solution)/shard_map/pack/pallas_call | solution.py:152
  3.8 14.2 %all-to-all-start = ((bf16[8,256,512]{2,1,0:T(8,128)(2,1)}), bf16[8,256,512]{2,1,0:T(8,128)(2,1)S(1)}, u32[]{:S(2)}, u32[]{:S(2)}) async-start(bf16[8,256,512]{2,1,0:T(8,128)(2,1)} %get-tuple-element.10), calls=%async_computation | async-start | bytes 4194304 | tf_op jit(solution)/shard_map/all_to_all | solution.py:144
  18.0 1.9 %collective-permute-start = (bf16[256,512]{1,0:T(8,128)(2,1)S(1)}, bf16[256,512]{1,0:T(8,128)(2,1)S(1)}, u32[]{:S(2)}, u32[]{:S(2)}) collective-permute-start(bf16[256,512]{1,0:T(8,128)(2,1)S(1)} %copy-done.2), channel_id=1, source_target_pairs={{96,3},{99,0},{3,96},{0,99},{100,7},{103,4},{7,100},{4,103},{104,1... | collective-permute-start | bytes 786440 | tf_op jit(solution)/shard_map/ppermute | solution.py:161
  19.9 1.3 %collective-permute-start.1 = (bf16[256,512]{1,0:T(8,128)(2,1)S(1)}, bf16[256,512]{1,0:T(8,128)(2,1)S(1)}, u32[]{:S(2)}, u32[]{:S(2)}) collective-permute-start(bf16[256,512]{1,0:T(8,128)(2,1)S(1)} %copy-done.2), channel_id=1, source_target_pairs={{96,2},{99,1},{3,97},{0,98},{100,6},{103,5},{7,101},{4,102},{104,1... | collective-permute-start | bytes 786440 | tf_op jit(solution)/shard_map/ppermute | solution.py:162
  21.2 7.6 %collective-permute-done = bf16[256,512]{1,0:T(8,128)(2,1)S(1)} collective-permute-done((bf16[256,512]{1,0:T(8,128)(2,1)S(1)}, bf16[256,512]{1,0:T(8,128)(2,1)S(1)}, u32[]{:S(2)}, u32[]{:S(2)}) %collective-permute-start) | collective-permute-done | bytes 262176 | tf_op jit(solution)/shard_map/ppermute | solution.py:161
  28.8 2.5 %collective-permute-done.1 = bf16[256,512]{1,0:T(8,128)(2,1)S(1)} collective-permute-done((bf16[256,512]{1,0:T(8,128)(2,1)S(1)}, bf16[256,512]{1,0:T(8,128)(2,1)S(1)}, u32[]{:S(2)}, u32[]{:S(2)}) %collective-permute-start.1) | collective-permute-done | bytes 262176 | tf_op jit(solution)/shard_map/ppermute | solution.py:162
  31.3 0.9 maximum_select_fusion.2
  32.2 2.6 %collective-permute-start.2 = (bf16[2,256,512]{2,1,0:T(8,128)(2,1)}, bf16[2,256,512]{2,1,0:T(8,128)(2,1)S(1)}, u32[]{:S(2)}, u32[]{:S(2)}) collective-permute-start(bf16[2,256,512]{2,1,0:T(8,128)(2,1)} %maximum_select_fusion.2), channel_id=1, source_target_pairs={{0,48},{48,0},{1,49},{49,1},{2,50},{50,2},{3,51},{51,3},{4,52},{52... | collective-permute-start | bytes 1572872 | tf_op jit(solution)/shard_map/ppermute | solution.py:165
  34.9 1.6 %collective-permute-done.2 = bf16[2,256,512]{2,1,0:T(8,128)(2,1)S(1)} collective-permute-done((bf16[2,256,512]{2,1,0:T(8,128)(2,1)}, bf16[2,256,512]{2,1,0:T(8,128)(2,1)S(1)}, u32[]{:S(2)}, u32[]{:S(2)}) %collective-permute-start.2) | collective-permute-done | bytes 524320 | tf_op jit(solution)/shard_map/ppermute | solution.py:165
  37.3 1.4 %maximum_select_fusion.pair = bf16[2,2,256,512]{3,2,1,0:T(8,128)(2,1)S(1)} fusion(bf16[1,2,256,512]{3,2,1,0:T(8,128)(2,1)} %bitcast.10, bf16[1,2,256,512]{3,2,1,0:T(8,128)(2,1)S(1)} %maximum_select_fusion.1, pred[]{:T(512)S(6)} %eq.12), kind=kLoop, calls=%fused_computation | loop fusion | flops 1572864 | bytes 2097153 | tf_op jit(solution)/shard_map/jit(_where)/select_n | solution.py:166
  38.7 5.6 %all-to-all-done.got = bf16[8,256,512]{2,1,0:T(8,128)(2,1)S(1)} async-done(((bf16[8,256,512]{2,1,0:T(8,128)(2,1)}), bf16[8,256,512]{2,1,0:T(8,128)(2,1)S(1)}, u32[]{:S(2)}, u32[]{:S(2)}) %all-to-all-start) | async-done | bytes 2097184 | tf_op jit(solution)/shard_map/all_to_all | solution.py:144
  44.3 0.9 grad.1
  45.2 0.9 convert_element_type.12
  46.1 4.4 %all-to-all-start.1 = ((f16[32,72,128]{2,1,0:T(8,128)(2,1)}), f16[32,72,128]{2,1,0:T(8,128)(2,1)S(1)}, u32[]{:S(2)}, u32[]{:S(2)}) async-start(f16[32,72,128]{2,1,0:T(8,128)(2,1)} %convert_element_type.12), calls=%async_computation.1 | async-start | bytes 1179648 | tf_op jit(solution)/shard_map/all_to_all | solution.py:144
  50.5 2.2 %collective-permute-start.3 = (bf16[2,2,256,512]{3,2,1,0:T(8,128)(2,1)S(1)}, bf16[2,2,256,512]{3,2,1,0:T(8,128)(2,1)}, u32[]{:S(2)}, u32[]{:S(2)}) collective-permute-start(bf16[2,2,256,512]{3,2,1,0:T(8,128)(2,1)S(1)} %get-tuple-element.12.w0), channel_id=1, source_target_pairs={{0,192},{192,384},{384,576},{576,0},{1,193},{193,385},{385,577},{5... | collective-permute-start | bytes 3145736 | tf_op jit(solution)/shard_map/ppermute | solution.py:174
  52.7 3.7 %collective-permute-start.4 = (bf16[2,2,256,512]{3,2,1,0:T(8,128)(2,1)S(1)}, bf16[2,2,256,512]{3,2,1,0:T(8,128)(2,1)}, u32[]{:S(2)}, u32[]{:S(2)}) collective-permute-start(bf16[2,2,256,512]{3,2,1,0:T(8,128)(2,1)S(1)} %get-tuple-element.12.w0), channel_id=1, source_target_pairs={{0,384},{192,576},{384,0},{576,192},{1,385},{193,577},{385,1},{577... | collective-permute-start | bytes 3145736 | tf_op jit(solution)/shard_map/ppermute | solution.py:174
  56.4 2.6 %collective-permute-start.5 = (bf16[2,2,256,512]{3,2,1,0:T(8,128)(2,1)S(1)}, bf16[2,2,256,512]{3,2,1,0:T(8,128)(2,1)}, u32[]{:S(2)}, u32[]{:S(2)}) collective-permute-start(bf16[2,2,256,512]{3,2,1,0:T(8,128)(2,1)S(1)} %get-tuple-element.12.w0), channel_id=1, source_target_pairs={{0,576},{192,0},{384,192},{576,384},{1,577},{193,1},{385,193},{577... | collective-permute-start | bytes 3145736 | tf_op jit(solution)/shard_map/ppermute | solution.py:174
  59.1 11.3 %all-to-all-done.1 = f16[32,72,128]{2,1,0:T(8,128)(2,1)S(1)} async-done(((f16[32,72,128]{2,1,0:T(8,128)(2,1)}), f16[32,72,128]{2,1,0:T(8,128)(2,1)S(1)}, u32[]{:S(2)}, u32[]{:S(2)}) %all-to-all-start.1) | async-done | bytes 589856 | tf_op jit(solution)/shard_map/all_to_all | solution.py:144
  70.6 17.9 %all_to_all.20.parts = f32[3,64,128]{2,1,0:T(8,128)S(1)} all-to-all(f32[3,64,128]{2,1,0:T(8,128)S(1)} %sum.1), channel_id=1, replica_groups=mesh['x'=4,'yh'=2,'core'=2,'zh'=3,'zl'=4,'yl'=4] {'zh'}, dimensions={0} | all-to-all | bytes 196608 | tf_op jit(solution)/shard_map/all_to_all | solution.py:144
  89.4 3.9 %all-to-all-start.3 = ((f16[16,72,128]{2,1,0:T(8,128)(2,1)}), f16[16,72,128]{2,1,0:T(8,128)(2,1)S(1)}, u32[]{:S(2)}, u32[]{:S(2)}) async-start(f16[16,72,128]{2,1,0:T(8,128)(2,1)} %convert_element_type.14), calls=%async_computation.3 | async-start | bytes 589824 | tf_op jit(solution)/shard_map/all_to_all | solution.py:144
  93.3 5.8 %collective-permute-done.4.w2 = bf16[2,2,256,512]{3,2,1,0:T(8,128)(2,1)} collective-permute-done((bf16[2,2,256,512]{3,2,1,0:T(8,128)(2,1)S(1)}, bf16[2,2,256,512]{3,2,1,0:T(8,128)(2,1)}, u32[]{:S(2)}, u32[]{:S(2)}) %collective-permute-start.4) | collective-permute-done | bytes 1048608 | tf_op jit(solution)/shard_map/ppermute | solution.py:174
  99.1 3.5 %collective-permute-done.5.w3 = bf16[2,2,256,512]{3,2,1,0:T(8,128)(2,1)} collective-permute-done((bf16[2,2,256,512]{3,2,1,0:T(8,128)(2,1)S(1)}, bf16[2,2,256,512]{3,2,1,0:T(8,128)(2,1)}, u32[]{:S(2)}, u32[]{:S(2)}) %collective-permute-start.5) | collective-permute-done | bytes 1048608 | tf_op jit(solution)/shard_map/ppermute | solution.py:174
  102.7 4.8 %project.1 = (bf16[128,512]{1,0:T(8,128)(2,1)}, bf16[128,4096]{1,0:T(8,128)(2,1)}) custom-call(s32[1]{0:T(128)} %bitcast.place, s32[1]{0:T(128)S(6)} %copy.9.counts, bf16[128,4096]{1,0:T(8,128)(2,1)S(1)} %copy-done, bf16[128,512]{1,0:T(8,128)(2,1)S(1)} %copy-done.1, f32[16,72,128]{2,1,0:T(8,128)S(1)} %final.1.after, ...), custom_call_target="tpu_custom_call" | custom-call | flops 1073741824 | bytes 6291456 | tf_op jit(solution)/shard_map/project/pallas_call | solution.py:181
  107.5 0.8 unpack.1
  (17 shorter events, 2.1 us)
Async XLA Ops:
  3.8 14.2 %copy-start.2 = (bf16[256,512]{1,0:T(8,128)(2,1)S(1)}, bf16[256,512]{1,0:T(8,128)(2,1)}, u32[]{:S(2)}) copy-start(bf16[256,512]{1,0:T(8,128)(2,1)} %param.6) | copy-start | bytes 786436
  3.8 40.5 %all-to-all-start = ((bf16[8,256,512]{2,1,0:T(8,128)(2,1)}), bf16[8,256,512]{2,1,0:T(8,128)(2,1)S(1)}, u32[]{:S(2)}, u32[]{:S(2)}) async-start(bf16[8,256,512]{2,1,0:T(8,128)(2,1)} %get-tuple-element.10), calls=%async_computation | async-start | bytes 4194304 | tf_op jit(solution)/shard_map/all_to_all | solution.py:144
  18.0 10.9 %collective-permute-start = (bf16[256,512]{1,0:T(8,128)(2,1)S(1)}, bf16[256,512]{1,0:T(8,128)(2,1)S(1)}, u32[]{:S(2)}, u32[]{:S(2)}) collective-permute-start(bf16[256,512]{1,0:T(8,128)(2,1)S(1)} %copy-done.2), channel_id=1, source_target_pairs={{96,3},{99,0},{3,96},{0,99},{100,7},{103,4},{7,100},{4,103},{104,1... | collective-permute-start | bytes 786440 | tf_op jit(solution)/shard_map/ppermute | solution.py:161
  19.9 11.4 %collective-permute-start.1 = (bf16[256,512]{1,0:T(8,128)(2,1)S(1)}, bf16[256,512]{1,0:T(8,128)(2,1)S(1)}, u32[]{:S(2)}, u32[]{:S(2)}) collective-permute-start(bf16[256,512]{1,0:T(8,128)(2,1)S(1)} %copy-done.2), channel_id=1, source_target_pairs={{96,2},{99,1},{3,97},{0,98},{100,6},{103,5},{7,101},{4,102},{104,1... | collective-permute-start | bytes 786440 | tf_op jit(solution)/shard_map/ppermute | solution.py:162
  32.2 4.3 %collective-permute-start.2 = (bf16[2,256,512]{2,1,0:T(8,128)(2,1)}, bf16[2,256,512]{2,1,0:T(8,128)(2,1)S(1)}, u32[]{:S(2)}, u32[]{:S(2)}) collective-permute-start(bf16[2,256,512]{2,1,0:T(8,128)(2,1)} %maximum_select_fusion.2), channel_id=1, source_target_pairs={{0,48},{48,0},{1,49},{49,1},{2,50},{50,2},{3,51},{51,3},{4,52},{52... | collective-permute-start | bytes 1572872 | tf_op jit(solution)/shard_map/ppermute | solution.py:165
  36.5 0.8 copy-start.3
  46.1 24.3 %all-to-all-start.1 = ((f16[32,72,128]{2,1,0:T(8,128)(2,1)}), f16[32,72,128]{2,1,0:T(8,128)(2,1)S(1)}, u32[]{:S(2)}, u32[]{:S(2)}) async-start(f16[32,72,128]{2,1,0:T(8,128)(2,1)} %convert_element_type.12), calls=%async_computation.1 | async-start | bytes 1179648 | tf_op jit(solution)/shard_map/all_to_all | solution.py:144
  50.5 42.8 %collective-permute-start.3 = (bf16[2,2,256,512]{3,2,1,0:T(8,128)(2,1)S(1)}, bf16[2,2,256,512]{3,2,1,0:T(8,128)(2,1)}, u32[]{:S(2)}, u32[]{:S(2)}) collective-permute-start(bf16[2,2,256,512]{3,2,1,0:T(8,128)(2,1)S(1)} %get-tuple-element.12.w0), channel_id=1, source_target_pairs={{0,192},{192,384},{384,576},{576,0},{1,193},{193,385},{385,577},{5... | collective-permute-start | bytes 3145736 | tf_op jit(solution)/shard_map/ppermute | solution.py:174
  52.7 46.4 %collective-permute-start.4 = (bf16[2,2,256,512]{3,2,1,0:T(8,128)(2,1)S(1)}, bf16[2,2,256,512]{3,2,1,0:T(8,128)(2,1)}, u32[]{:S(2)}, u32[]{:S(2)}) collective-permute-start(bf16[2,2,256,512]{3,2,1,0:T(8,128)(2,1)S(1)} %get-tuple-element.12.w0), channel_id=1, source_target_pairs={{0,384},{192,576},{384,0},{576,192},{1,385},{193,577},{385,1},{577... | collective-permute-start | bytes 3145736 | tf_op jit(solution)/shard_map/ppermute | solution.py:174
  56.4 46.2 %collective-permute-start.5 = (bf16[2,2,256,512]{3,2,1,0:T(8,128)(2,1)S(1)}, bf16[2,2,256,512]{3,2,1,0:T(8,128)(2,1)}, u32[]{:S(2)}, u32[]{:S(2)}) collective-permute-start(bf16[2,2,256,512]{3,2,1,0:T(8,128)(2,1)S(1)} %get-tuple-element.12.w0), channel_id=1, source_target_pairs={{0,576},{192,0},{384,192},{576,384},{1,577},{193,1},{385,193},{577... | collective-permute-start | bytes 3145736 | tf_op jit(solution)/shard_map/ppermute | solution.py:174
  70.5 32.2 %copy-start = (bf16[128,4096]{1,0:T(8,128)(2,1)S(1)}, bf16[128,4096]{1,0:T(8,128)(2,1)}, u32[]{:S(2)}) copy-start(bf16[128,4096]{1,0:T(8,128)(2,1)} %acts.3) | copy-start | bytes 3145732
  70.5 32.2 %copy-start.1 = (bf16[128,512]{1,0:T(8,128)(2,1)S(1)}, bf16[128,512]{1,0:T(8,128)(2,1)}, u32[]{:S(2)}) copy-start(bf16[128,512]{1,0:T(8,128)(2,1)} %get-tuple-element.9.masked) | copy-start | bytes 393220
  89.4 18.0 %all-to-all-start.3 = ((f16[16,72,128]{2,1,0:T(8,128)(2,1)}), f16[16,72,128]{2,1,0:T(8,128)(2,1)S(1)}, u32[]{:S(2)}, u32[]{:S(2)}) async-start(f16[16,72,128]{2,1,0:T(8,128)(2,1)} %convert_element_type.14), calls=%async_computation.3 | async-start | bytes 589824 | tf_op jit(solution)/shard_map/all_to_all | solution.py:144

commit v3 on v2

--- a/solution.py
+++ b/solution.py
@@ -12,6 +12,7 @@
 TOK, DIN, HD = 128, 4096, 512
 SHARD = DIN // (X * YH * CORE)
 PEERS = X * CORE
+HALF = DIN // CORE
 PIECES = YH * ZL * YL
 ROWS = SHARD // (ZL * YL)
 LANES = 128
@@ -19,6 +20,7 @@
 TALL = FLAT + 8
 SCALE = float(TOK * X * YH * CORE * ZH * ZL * YL) ** -0.5
 TOP = 13.0
+SWAP = [(0, 1), (1, 0)]
 
 VMEM = pl.BlockSpec(memory_space=pltpu.VMEM)
 SMEM = pl.BlockSpec(memory_space=pltpu.SMEM)
@@ -27,8 +29,9 @@
 bf16, f16, f32 = jnp.bfloat16, jnp.float16, jnp.float32
 
 
-def pack_kernel(counts, acts, cot, packed, masked, raw, kept, full, built, sems):
+def pack_kernel(place, counts, acts, cot, packed, masked, lend, raw, kept, full, built, loan, sems):
     wide = DIN // X
+    away = 1 - place[0]
     first = pltpu.make_async_copy(cot, raw, sems.at[0])
     first.start()
     loads = [
@@ -51,9 +54,15 @@
                 b = (x * YH + yh) * CORE + side
                 built[peer, 0:TOK, yh * SHARD:(yh + 1) * SHARD] = full[:, b * SHARD:(b + 1) * SHARD]
             built[peer, TOK:2 * TOK, :] = kept[...]
+        for yh in range(YH):
+            start = pl.multiple_of(((x * YH + yh) * CORE + away) * SHARD, SHARD)
+            loan[:, (x * YH + yh) * SHARD:(x * YH + yh + 1) * SHARD] = full[:, pl.ds(start, SHARD)]
         pieces = slice(x * CORE, (x + 1) * CORE)
         stores.append(pltpu.make_async_copy(built.at[pieces], packed.at[pieces], sems.at[2 + X + x]))
         stores[-1].start()
+    loan[:, HALF:HALF + HD] = kept[...]
+    stores.append(pltpu.make_async_copy(loan, lend, sems.at[2 + 2 * X]))
+    stores[-1].start()
     for store in stores:
         store.wait()
 
@@ -73,7 +82,7 @@
     return ref[i, 0:FLAT, :] * jnp.exp2(-ref[i, FLAT:FLAT + 1, :])
 
 
-def grad_kernel(got, pair, out, same, acc):
+def grad_kernel(got, pair, loan, out, same, same_loan, acc):
     cols = 128
     right = got[:, TOK:2 * TOK, :].reshape(PEERS * TOK, HD)
     for i in range(YH * SHARD // cols):
@@ -113,21 +122,43 @@
             out[i * ROWS:(i + 1) * ROWS, j * LANES:(j + 1) * LANES] = value[j * ROWS:(j + 1) * ROWS, :]
 
 
-def project_kernel(place, counts, acts, masked, after, w0, w1, w2, w3, projected, act_grad):
-    x = place[0]
-    kept = masked[...]
-    total = jnp.zeros((TOK, HD), f32)
+def project_kernel(place, acts, masked, loan, after, w0, w1, w2, w3, part, grad, grad_away):
+    x, core = place[0], place[1]
+    kept = jnp.concatenate([masked[...], loan[:, HALF:HALF + HD]], axis=0)
+    total = jnp.zeros((2 * TOK, HD), f32)
     for k, shards in enumerate((w0, w1, w2, w3)):
-        group = lax.rem(x - k + X, X) * YH * CORE
-        for core in range(CORE):
-            for yh in range(YH):
-                w = shards[core, yh]
-                start = pl.multiple_of((group + yh * CORE + core) * SHARD, SHARD)
-                total += jnp.dot(acts[:, pl.ds(start, SHARD)], w, preferred_element_type=f32)
-                back = lax.dot_general(kept, w, (((1,), (1,)), ((), ())), preferred_element_type=f32)
-                act_grad[:, pl.ds(start, SHARD)] = back.astype(bf16)
+        group = lax.rem(x - k + X, X) * YH
+        for yh in range(YH):
+            w = shards[yh]
+            near = pl.multiple_of(((group + yh) * CORE + core) * SHARD, SHARD)
+            far = pl.multiple_of((group + yh) * SHARD, SHARD)
+            rows = jnp.concatenate([acts[:, pl.ds(near, SHARD)], loan[:, pl.ds(far, SHARD)]], axis=0)
+            total += jnp.dot(rows, w, preferred_element_type=f32)
+            back = lax.dot_general(kept, w, (((1,), (1,)), ((), ())), preferred_element_type=f32).astype(bf16)
+            cols = slice((k * YH + yh) * SHARD, (k * YH + yh + 1) * SHARD)
+            grad[:, cols] = back[0:TOK]
+            grad_away[:, cols] = back[TOK:2 * TOK]
+    part[...] = total[0:TOK]
+    top = total[TOK:2 * TOK].astype(bf16)
+    grad_away[:, HALF:HALF + HD] = top
+    grad_away[:, HALF + HD:HALF + 2 * HD] = (total[TOK:2 * TOK] - top.astype(f32)).astype(bf16)
+
+
+def join_kernel(place, counts, part, grad, grad_away, projected, act_grad):
+    x, core = place[0], place[1]
     rows = lax.broadcasted_iota(jnp.int32, (TOK, HD), 0)
+    top = grad_away[:, HALF:HALF + HD].astype(f32)
+    rest = grad_away[:, HALF + HD:HALF + 2 * HD].astype(f32)
+    total = part[...] + (top + rest)
     projected[...] = jnp.where(rows < counts[0] * MICRO, total, 0.0).astype(bf16)
+    for k in range(X):
+        group = lax.rem(x - k + X, X) * YH
+        for yh in range(YH):
+            cols = slice((k * YH + yh) * SHARD, (k * YH + yh + 1) * SHARD)
+            near = pl.multiple_of(((group + yh) * CORE + core) * SHARD, SHARD)
+            far = pl.multiple_of(((group + yh) * CORE + 1 - core) * SHARD, SHARD)
+            act_grad[:, pl.ds(near, SHARD)] = grad[:, cols]
+            act_grad[:, pl.ds(far, SHARD)] = grad_away[:, cols]
 
 
 def sds(shape, dtype):
@@ -149,41 +180,50 @@
     yh, yl = lax.axis_index("yh"), lax.axis_index("yl")
     dma = pltpu.SemaphoreType.DMA
 
-    packed, masked = call(
-        pack_kernel, (sds((PEERS, 2 * TOK, HD), bf16), sds((TOK, HD), bf16)),
-        [SMEM, ANY, ANY], (ANY, ANY),
+    packed, masked, lend = call(
+        pack_kernel,
+        (sds((PEERS, 2 * TOK, HD), bf16), sds((TOK, HD), bf16), sds((TOK, HALF + HD), bf16)),
+        [SMEM, SMEM, ANY, ANY], (ANY, ANY, ANY),
         (pltpu.VMEM((TOK, HD), bf16), pltpu.VMEM((TOK, HD), bf16), pltpu.VMEM((TOK, DIN), bf16),
-         pltpu.VMEM((PEERS, 2 * TOK, HD), bf16), dma((2 + 2 * X,))),
+         pltpu.VMEM((PEERS, 2 * TOK, HD), bf16), pltpu.VMEM((TOK, HALF + HD), bf16), dma((3 + 2 * X,))),
         "pack", LARGE,
-    )(batch_counts, acts, cotangent)
+    )(core.reshape(1), batch_counts, acts, cotangent)
     got = exchange(packed, ("x", "core"))
 
     near = lax.ppermute(kv_weight, ("yh", "yl"), [(4, 3), (7, 0), (3, 4), (0, 7)])
     far = lax.ppermute(kv_weight, ("yh", "yl"), [(4, 2), (7, 1), (3, 5), (0, 6)])
     twin = jnp.where((yl == 0) | (yl == YL - 1), near, far)
     pair = jnp.where(yh == 0, jnp.stack([kv_weight, twin]), jnp.stack([twin, kv_weight]))
-    side = lax.ppermute(pair, "core", [(0, 1), (1, 0)])
-    quad = jnp.where(core == 0, jnp.stack([pair, side]), jnp.stack([side, pair]))
-
-    partial, quad = call(
-        grad_kernel, (sds((PIECES, TALL, LANES), f32), sds((CORE, YH, SHARD, HD), bf16)),
-        [VMEM, ANY], (VMEM, ANY), (pltpu.VMEM((YH * SHARD, HD), f32),), "grad",
-        input_output_aliases={1: 1},
-    )(got, quad)
+    loan = lax.ppermute(lend, "core", SWAP)
+
+    partial, pair, loan = call(
+        grad_kernel,
+        (sds((PIECES, TALL, LANES), f32), sds((YH, SHARD, HD), bf16), sds((TOK, HALF + HD), bf16)),
+        [VMEM, ANY, ANY], (VMEM, ANY, ANY), (pltpu.VMEM((YH * SHARD, HD), f32),), "grad",
+        input_output_aliases={1: 1, 2: 2},
+    )(got, pair, loan)
+
     parts = exchange(partial.astype(f16), ("yh", "zl", "yl"))
-    turned = [lax.ppermute(quad, "x", [(i, (i + k) % X) for i in range(X)]) for k in range(1, X)]
+    turned = [lax.ppermute(pair, "x", [(i, (i + k) % X) for i in range(X)]) for k in range(1, X)]
     piece = call(sum_kernel, sds((ZH, FLAT, LANES), f32), [VMEM], VMEM, name="sum", limit=TINY)(parts.astype(f32))
     pieces = exchange(piece, "zh")
     ready = call(
         final_kernel, sds((ZL * YL, TALL, LANES), f32), [VMEM], VMEM, name="final", limit=TINY)(pieces)
     whole = exchange(ready.astype(f16), ("zl", "yl"))
 
-    projected, act_grad = call(
-        project_kernel, (sds((TOK, HD), bf16), sds((TOK, DIN), bf16)),
-        [SMEM, SMEM, VMEM, VMEM, ANY] + [VMEM] * 4, (VMEM, VMEM), (), "project", SMALL,
+    place = jnp.stack([x, core])
+    part, grad, grad_away = call(
+        project_kernel,
+        (sds((TOK, HD), f32), sds((TOK, HALF), bf16), sds((TOK, HALF + 2 * HD), bf16)),
+        [SMEM, VMEM, VMEM, VMEM, ANY] + [VMEM] * 4, (VMEM,) * 3, (), "project", SMALL,
         cost_estimate=pl.CostEstimate(
             flops=4 * TOK * DIN * HD, bytes_accessed=2 * (2 * TOK * DIN + DIN * HD), transcendentals=0),
-    )(x.reshape(1), batch_counts, acts, masked, ready, quad, *turned)
+    )(place, acts, masked, loan, piece, pair, *turned)
+    grad_away = lax.ppermute(grad_away, "core", SWAP)
+    projected, act_grad = call(
+        join_kernel, (sds((TOK, HD), bf16), sds((TOK, DIN), bf16)),
+        [SMEM, SMEM] + [VMEM] * 3, (VMEM, VMEM), (), "join", SMALL,
+    )(place, batch_counts, part, grad, grad_away)
 
     weight_grad = call(
         unpack_kernel, sds((SHARD, HD), f32), [VMEM], VMEM, name="unpack", limit=TINY)(whole.astype(f32))

time: 109 us -> 107 us (0.982)
  blocking collectives: 17.9 us -> 0 us
  starting transfers between devices: 36.8 us -> 51.5 us
  waiting for transfers between devices: 38 us -> 41.8 us
  other arithmetic: 4.15 us -> 1.95 us
    all_to_all x1 -> x0, blocking collectives: 17.9 us -> none  [exchange(): return lax.all_to_all(value, axes, 0, 0, tiled=True)]
    all_to_all x3 -> x4, waiting for transfers between devices: 16.9 us -> 30.7 us  [exchange(): return lax.all_to_all(value, axes, 0, 0, tiled=True)]
    all_to_all x3 -> x4, starting transfers between devices: 22.4 us -> 33.4 us  [exchange(): return lax.all_to_all(value, axes, 0, 0, tiled=True)]
    ppermute x4 -> x5, waiting for transfers between devices: 11 us -> 1.9 us  [the longest x1 1.89 us: per_device(): grad_away = lax.ppermute(grad_away, 'core', SWAP)]
    ppermute x4 -> x5, starting transfers between devices: 11.1 us -> 14.9 us  [the longest x3 7.81 us: per_device(): lax.ppermute(pair, 'x', [(i, (i + k) % X) for i in range(X)])]
    ppermute x1, waiting for transfers between devices: 7.62 us -> 5.62 us  [per_device(): lax.ppermute(kv_weight, ('yh', 'yl'), [(4, 3), (7, 0), (3, 4), (0, 7)])]
    select_n x1 -> x0, other arithmetic: 1.39 us -> none  [per_device(): jnp.where(core == 0, jnp.stack([pair, side]), jnp.stack([side, pair]))]
    ppermute x1, waiting for transfers between devices: 2.47 us -> 3.64 us  [per_device(): lax.ppermute(kv_weight, ('yh', 'yl'), [(4, 2), (7, 1), (3, 5), (0, 6)])]
  transfers between devices with their start and end apart: 9 -> 11, of which waited for: 7 -> 6; matrix products, arithmetic and copies ran while one was open for 3% -> 1% of each run, Pallas kernels for 5% -> 5%
where the time goes in v3:
time: 107 us; the launch traced here: 106 us
  starting transfers between devices  51.5 us (48%)
  waiting for transfers between devices  41.8 us (39%)
  Pallas kernels  9.64 us (9%)
  other arithmetic  1.95 us (2%)
  between operations  1.5 us (1%)
    all_to_all x4, starting transfers between devices, exchange(): return lax.all_to_all(value, axes, 0, 0, tiled=True)  33.4 us
    all_to_all x4, waiting for transfers between devices, exchange(): return lax.all_to_all(value, axes, 0, 0, tiled=True)  30.7 us
    ppermute x3, starting transfers between devices, per_device(): lax.ppermute(pair, 'x', [(i, (i + k) % X) for i in range(X)])  7.81 us
    ppermute x1, waiting for transfers between devices, per_device(): lax.ppermute(kv_weight, ('yh', 'yl'), [(4, 3), (7, 0), (3, 4), (0, 7)])  5.62 us
    ppermute x1, starting transfers between devices, per_device(): grad_away = lax.ppermute(grad_away, 'core', SWAP)  5.08 us
    ppermute x1, waiting for transfers between devices, per_device(): lax.ppermute(kv_weight, ('yh', 'yl'), [(4, 2), (7, 1), (3, 5), (0, 6)])  3.64 us
    pallas_call x1, Pallas kernels, per_device(): call(pack_kernel, (sds((PEERS, 2 * TOK, HD), bf16), sds((TOK, HD), bf16),...  2.68 us
    pallas_call x1, Pallas kernels, per_device(): call(project_kernel, (sds((TOK, HD), f32), sds((TOK, HALF), bf16), sds((T...  2.65 us
  transfers between devices with their start and end apart: 11, of which 6 were waited for; matrix products, arithmetic and copies ran while one was open for 1% of the time, Pallas kernels for 5%

profile of v3, /device:TPU:1, one launch (start us, length us, event | category | flops | bytes accessed | tf_op | source)
XLA Modules:
  0.0 106.5 jit_solution(10728988040509431696)
XLA Ops:
  1.3 2.7 %pack.1 = (bf16[8,256,512]{2,1,0:T(8,128)(2,1)}, bf16[128,512]{1,0:T(8,128)(2,1)}, bf16[128,2560]{1,0:T(8,128)(2,1)}) custom-call(s32[1]{0:T(128)} %bitcast.1.place, s32[1]{0:T(128)S(6)} %copy.11.counts, bf16[128,4096]{1,0:T(8,128)(2,1)} %acts.3, bf16[128,512]{1,0:T(8,128)(2,1)} %cot.1), custom_call_target="tpu_custom_call" | custom-call | tf_op jit(solution)/shard_map/pack/pallas_call | solution.py:183
  4.0 14.2 %all-to-all-start = ((bf16[8,256,512]{2,1,0:T(8,128)(2,1)}), bf16[8,256,512]{2,1,0:T(8,128)(2,1)S(1)}, u32[]{:S(2)}, u32[]{:S(2)}) async-start(bf16[8,256,512]{2,1,0:T(8,128)(2,1)} %get-tuple-element.15), calls=%async_computation | async-start | bytes 4194304 | tf_op jit(solution)/shard_map/all_to_all | solution.py:175
  18.1 2.0 %collective-permute-start.2 = (bf16[128,2560]{1,0:T(8,128)(2,1)}, bf16[128,2560]{1,0:T(8,128)(2,1)S(1)}, u32[]{:S(2)}, u32[]{:S(2)}) collective-permute-start(bf16[128,2560]{1,0:T(8,128)(2,1)} %get-tuple-element.16), channel_id=1, source_target_pairs={{0,48},{48,0},{1,49},{49,1},{2,50},{50,2},{3,51},{51,3},{4,52},{52... | collective-permute-start | bytes 1966088 | tf_op jit(solution)/shard_map/ppermute | solution.py:197
  20.2 1.3 %collective-permute-start.1 = (bf16[256,512]{1,0:T(8,128)(2,1)S(1)}, bf16[256,512]{1,0:T(8,128)(2,1)S(1)}, u32[]{:S(2)}, u32[]{:S(2)}) collective-permute-start(bf16[256,512]{1,0:T(8,128)(2,1)S(1)} %copy-done.2), channel_id=1, source_target_pairs={{96,2},{99,1},{3,97},{0,98},{100,6},{103,5},{7,101},{4,102},{104,1... | collective-permute-start | bytes 786440 | tf_op jit(solution)/shard_map/ppermute | solution.py:194
  21.5 1.9 %collective-permute-start = (bf16[256,512]{1,0:T(8,128)(2,1)S(1)}, bf16[256,512]{1,0:T(8,128)(2,1)S(1)}, u32[]{:S(2)}, u32[]{:S(2)}) collective-permute-start(bf16[256,512]{1,0:T(8,128)(2,1)S(1)} %copy-done.2), channel_id=1, source_target_pairs={{96,3},{99,0},{3,96},{0,99},{100,7},{103,4},{7,100},{4,103},{104,1... | collective-permute-start | bytes 786440 | tf_op jit(solution)/shard_map/ppermute | solution.py:193
  23.4 3.6 %collective-permute-done.1 = bf16[256,512]{1,0:T(8,128)(2,1)S(1)} collective-permute-done((bf16[256,512]{1,0:T(8,128)(2,1)S(1)}, bf16[256,512]{1,0:T(8,128)(2,1)S(1)}, u32[]{:S(2)}, u32[]{:S(2)}) %collective-permute-start.1) | collective-permute-done | bytes 262176 | tf_op jit(solution)/shard_map/ppermute | solution.py:194
  27.1 5.6 %collective-permute-done = bf16[256,512]{1,0:T(8,128)(2,1)S(1)} collective-permute-done((bf16[256,512]{1,0:T(8,128)(2,1)S(1)}, bf16[256,512]{1,0:T(8,128)(2,1)S(1)}, u32[]{:S(2)}, u32[]{:S(2)}) %collective-permute-start) | collective-permute-done | bytes 262176 | tf_op jit(solution)/shard_map/ppermute | solution.py:193
  32.8 11.7 %all-to-all-done.got = bf16[8,256,512]{2,1,0:T(8,128)(2,1)S(1)} async-done(((bf16[8,256,512]{2,1,0:T(8,128)(2,1)}), bf16[8,256,512]{2,1,0:T(8,128)(2,1)S(1)}, u32[]{:S(2)}, u32[]{:S(2)}) %all-to-all-start) | async-done | bytes 2097184 | tf_op jit(solution)/shard_map/all_to_all | solution.py:175
  44.5 0.9 grad.1
  45.4 0.9 convert_element_type.12
  46.3 4.4 %all-to-all-start.1 = ((f16[32,72,128]{2,1,0:T(8,128)(2,1)}), f16[32,72,128]{2,1,0:T(8,128)(2,1)S(1)}, u32[]{:S(2)}, u32[]{:S(2)}) async-start(f16[32,72,128]{2,1,0:T(8,128)(2,1)} %convert_element_type.12), calls=%async_computation.1 | async-start | bytes 1179648 | tf_op jit(solution)/shard_map/all_to_all | solution.py:175
  50.7 2.8 %collective-permute-start.5 = (bf16[2,256,512]{2,1,0:T(8,128)(2,1)S(1)}, bf16[2,256,512]{2,1,0:T(8,128)(2,1)}, u32[]{:S(2)}, u32[]{:S(2)}) collective-permute-start(bf16[2,256,512]{2,1,0:T(8,128)(2,1)S(1)} %get-tuple-element.19.w0), channel_id=1, source_target_pairs={{0,576},{192,0},{384,192},{576,384},{1,577},{193,1},{385,193},{577... | collective-permute-start | bytes 1572872 | tf_op jit(solution)/shard_map/ppermute | solution.py:207
  53.5 3.1 %collective-permute-start.4 = (bf16[2,256,512]{2,1,0:T(8,128)(2,1)S(1)}, bf16[2,256,512]{2,1,0:T(8,128)(2,1)}, u32[]{:S(2)}, u32[]{:S(2)}) collective-permute-start(bf16[2,256,512]{2,1,0:T(8,128)(2,1)S(1)} %get-tuple-element.19.w0), channel_id=1, source_target_pairs={{0,384},{192,576},{384,0},{576,192},{1,385},{193,577},{385,1},{577... | collective-permute-start | bytes 1572872 | tf_op jit(solution)/shard_map/ppermute | solution.py:207
  56.6 1.9 %collective-permute-start.3 = (bf16[2,256,512]{2,1,0:T(8,128)(2,1)S(1)}, bf16[2,256,512]{2,1,0:T(8,128)(2,1)}, u32[]{:S(2)}, u32[]{:S(2)}) collective-permute-start(bf16[2,256,512]{2,1,0:T(8,128)(2,1)S(1)} %get-tuple-element.19.w0), channel_id=1, source_target_pairs={{0,192},{192,384},{384,576},{576,0},{1,193},{193,385},{385,577},{5... | collective-permute-start | bytes 1572872 | tf_op jit(solution)/shard_map/ppermute | solution.py:207
  58.6 12.0 %all-to-all-done.1 = f16[32,72,128]{2,1,0:T(8,128)(2,1)S(1)} async-done(((f16[32,72,128]{2,1,0:T(8,128)(2,1)}), f16[32,72,128]{2,1,0:T(8,128)(2,1)S(1)}, u32[]{:S(2)}, u32[]{:S(2)}) %all-to-all-start.1) | async-done | bytes 589856 | tf_op jit(solution)/shard_map/all_to_all | solution.py:175
  71.5 10.9 %all-to-all-start.2 = ((f32[3,64,128]{2,1,0:T(8,128)}), f32[3,64,128]{2,1,0:T(8,128)S(1)}, u32[]{:S(2)}, u32[]{:S(2)}) async-start(f32[3,64,128]{2,1,0:T(8,128)} %sum.1.after), calls=%async_computation.2 | async-start | bytes 196608 | tf_op jit(solution)/shard_map/all_to_all | solution.py:175
  82.5 6.9 %all-to-all-done.2.parts = f32[3,64,128]{2,1,0:T(8,128)S(1)} async-done(((f32[3,64,128]{2,1,0:T(8,128)}), f32[3,64,128]{2,1,0:T(8,128)S(1)}, u32[]{:S(2)}, u32[]{:S(2)}) %all-to-all-start.2) | async-done | bytes 98336 | tf_op jit(solution)/shard_map/all_to_all | solution.py:175
  89.6 0.8 convert_element_type.14
  90.3 3.9 %all-to-all-start.3 = ((f16[16,72,128]{2,1,0:T(8,128)(2,1)}), f16[16,72,128]{2,1,0:T(8,128)(2,1)S(1)}, u32[]{:S(2)}, u32[]{:S(2)}) async-start(f16[16,72,128]{2,1,0:T(8,128)(2,1)} %convert_element_type.14), calls=%async_computation.3 | async-start | bytes 589824 | tf_op jit(solution)/shard_map/all_to_all | solution.py:175
  94.3 2.6 %project.1 = (f32[128,512]{1,0:T(8,128)S(1)}, bf16[128,2048]{1,0:T(8,128)(2,1)S(1)}, bf16[128,3072]{1,0:T(8,128)(2,1)S(1)}) custom-call(s32[2]{0:T(128)S(1)} %pad_add_fusion.place, bf16[128,4096]{1,0:T(8,128)(2,1)S(1)} %copy-done, bf16[128,512]{1,0:T(8,128)(2,1)S(1)} %copy-done.1, bf16[128,2560]{1,0:T(8,128)(2,1)S(1)} %get-tuple-element.17.loan, ...), custom_call_target="tpu_custom_call" | custom-call | flops 1073741824 | bytes 6291456 | tf_op jit(solution)/shard_map/project/pallas_call | solution.py:215
  96.9 5.1 %collective-permute-start.6 = (bf16[128,3072]{1,0:T(8,128)(2,1)S(1)}, bf16[128,3072]{1,0:T(8,128)(2,1)S(1)}, u32[]{:S(2)}, u32[]{:S(2)}) collective-permute-start(bf16[128,3072]{1,0:T(8,128)(2,1)S(1)} %get-tuple-element.22), channel_id=1, source_target_pairs={{0,48},{48,0},{1,49},{49,1},{2,50},{50,2},{3,51},{51,3},{4,52},{52... | collective-permute-start | bytes 2359304 | tf_op jit(solution)/shard_map/ppermute | solution.py:222
  102.0 1.9 %collective-permute-done.6.grad_away = bf16[128,3072]{1,0:T(8,128)(2,1)S(1)} collective-permute-done((bf16[128,3072]{1,0:T(8,128)(2,1)S(1)}, bf16[128,3072]{1,0:T(8,128)(2,1)S(1)}, u32[]{:S(2)}, u32[]{:S(2)}) %collective-permute-start.6) | collective-permute-done | bytes 786464 | tf_op jit(solution)/shard_map/ppermute | solution.py:222
  103.9 1.7 %join.1 = (bf16[128,512]{1,0:T(8,128)(2,1)}, bf16[128,4096]{1,0:T(8,128)(2,1)}) custom-call(s32[2]{0:T(128)S(1)} %pad_add_fusion.place, s32[1]{0:T(128)S(6)} %copy.11.counts, f32[128,512]{1,0:T(8,128)S(1)} %get-tuple-element.20.part, bf16[128,2048]{1,0:T(8,128)(2,1)S(1)} %get-tuple-element.21.grad, bf16[128,3072]{1,0:T(8,128)(2,1)S(1)} %collective-permute-done.6.grad_away), custom_call_target="tpu_custom_call" | custom-call | tf_op jit(solution)/shard_map/join/pallas_call | solution.py:223
  105.6 0.8 unpack.1
  (18 shorter events, 1.2 us)
Async XLA Ops:
  4.0 16.2 %copy-start.2 = (bf16[256,512]{1,0:T(8,128)(2,1)S(1)}, bf16[256,512]{1,0:T(8,128)(2,1)}, u32[]{:S(2)}) copy-start(bf16[256,512]{1,0:T(8,128)(2,1)} %param.6) | copy-start | bytes 786436
  4.0 40.5 %all-to-all-start = ((bf16[8,256,512]{2,1,0:T(8,128)(2,1)}), bf16[8,256,512]{2,1,0:T(8,128)(2,1)S(1)}, u32[]{:S(2)}, u32[]{:S(2)}) async-start(bf16[8,256,512]{2,1,0:T(8,128)(2,1)} %get-tuple-element.15), calls=%async_computation | async-start | bytes 4194304 | tf_op jit(solution)/shard_map/all_to_all | solution.py:175
  18.1 14.7 %collective-permute-start.2 = (bf16[128,2560]{1,0:T(8,128)(2,1)}, bf16[128,2560]{1,0:T(8,128)(2,1)S(1)}, u32[]{:S(2)}, u32[]{:S(2)}) collective-permute-start(bf16[128,2560]{1,0:T(8,128)(2,1)} %get-tuple-element.16), channel_id=1, source_target_pairs={{0,48},{48,0},{1,49},{49,1},{2,50},{50,2},{3,51},{51,3},{4,52},{52... | collective-permute-start | bytes 1966088 | tf_op jit(solution)/shard_map/ppermute | solution.py:197
  20.2 6.9 %collective-permute-start.1 = (bf16[256,512]{1,0:T(8,128)(2,1)S(1)}, bf16[256,512]{1,0:T(8,128)(2,1)S(1)}, u32[]{:S(2)}, u32[]{:S(2)}) collective-permute-start(bf16[256,512]{1,0:T(8,128)(2,1)S(1)} %copy-done.2), channel_id=1, source_target_pairs={{96,2},{99,1},{3,97},{0,98},{100,6},{103,5},{7,101},{4,102},{104,1... | collective-permute-start | bytes 786440 | tf_op jit(solution)/shard_map/ppermute | solution.py:194
  21.5 11.2 %collective-permute-start = (bf16[256,512]{1,0:T(8,128)(2,1)S(1)}, bf16[256,512]{1,0:T(8,128)(2,1)S(1)}, u32[]{:S(2)}, u32[]{:S(2)}) collective-permute-start(bf16[256,512]{1,0:T(8,128)(2,1)S(1)} %copy-done.2), channel_id=1, source_target_pairs={{96,3},{99,0},{3,96},{0,99},{100,7},{103,4},{7,100},{4,103},{104,1... | collective-permute-start | bytes 786440 | tf_op jit(solution)/shard_map/ppermute | solution.py:193
  46.3 24.3 %all-to-all-start.1 = ((f16[32,72,128]{2,1,0:T(8,128)(2,1)}), f16[32,72,128]{2,1,0:T(8,128)(2,1)S(1)}, u32[]{:S(2)}, u32[]{:S(2)}) async-start(f16[32,72,128]{2,1,0:T(8,128)(2,1)} %convert_element_type.12), calls=%async_computation.1 | async-start | bytes 1179648 | tf_op jit(solution)/shard_map/all_to_all | solution.py:175
  50.7 43.5 %collective-permute-start.5 = (bf16[2,256,512]{2,1,0:T(8,128)(2,1)S(1)}, bf16[2,256,512]{2,1,0:T(8,128)(2,1)}, u32[]{:S(2)}, u32[]{:S(2)}) collective-permute-start(bf16[2,256,512]{2,1,0:T(8,128)(2,1)S(1)} %get-tuple-element.19.w0), channel_id=1, source_target_pairs={{0,576},{192,0},{384,192},{576,384},{1,577},{193,1},{385,193},{577... | collective-permute-start | bytes 1572872 | tf_op jit(solution)/shard_map/ppermute | solution.py:207
  53.5 40.7 %collective-permute-start.4 = (bf16[2,256,512]{2,1,0:T(8,128)(2,1)S(1)}, bf16[2,256,512]{2,1,0:T(8,128)(2,1)}, u32[]{:S(2)}, u32[]{:S(2)}) collective-permute-start(bf16[2,256,512]{2,1,0:T(8,128)(2,1)S(1)} %get-tuple-element.19.w0), channel_id=1, source_target_pairs={{0,384},{192,576},{384,0},{576,192},{1,385},{193,577},{385,1},{577... | collective-permute-start | bytes 1572872 | tf_op jit(solution)/shard_map/ppermute | solution.py:207
  56.6 37.6 %collective-permute-start.3 = (bf16[2,256,512]{2,1,0:T(8,128)(2,1)S(1)}, bf16[2,256,512]{2,1,0:T(8,128)(2,1)}, u32[]{:S(2)}, u32[]{:S(2)}) collective-permute-start(bf16[2,256,512]{2,1,0:T(8,128)(2,1)S(1)} %get-tuple-element.19.w0), channel_id=1, source_target_pairs={{0,192},{192,384},{384,576},{576,0},{1,193},{193,385},{385,577},{5... | collective-permute-start | bytes 1572872 | tf_op jit(solution)/shard_map/ppermute | solution.py:207
  70.7 23.6 %copy-start = (bf16[128,4096]{1,0:T(8,128)(2,1)S(1)}, bf16[128,4096]{1,0:T(8,128)(2,1)}, u32[]{:S(2)}) copy-start(bf16[128,4096]{1,0:T(8,128)(2,1)} %acts.3) | copy-start | bytes 3145732
  70.7 23.6 %copy-start.1 = (bf16[128,512]{1,0:T(8,128)(2,1)S(1)}, bf16[128,512]{1,0:T(8,128)(2,1)}, u32[]{:S(2)}) copy-start(bf16[128,512]{1,0:T(8,128)(2,1)} %get-tuple-element.14.masked) | copy-start | bytes 393220
  71.5 18.0 %all-to-all-start.2 = ((f32[3,64,128]{2,1,0:T(8,128)}), f32[3,64,128]{2,1,0:T(8,128)S(1)}, u32[]{:S(2)}, u32[]{:S(2)}) async-start(f32[3,64,128]{2,1,0:T(8,128)} %sum.1.after), calls=%async_computation.2 | async-start | bytes 196608 | tf_op jit(solution)/shard_map/all_to_all | solution.py:175
  90.3 15.3 %all-to-all-start.3 = ((f16[16,72,128]{2,1,0:T(8,128)(2,1)}), f16[16,72,128]{2,1,0:T(8,128)(2,1)S(1)}, u32[]{:S(2)}, u32[]{:S(2)}) async-start(f16[16,72,128]{2,1,0:T(8,128)(2,1)} %convert_element_type.14), calls=%async_computation.3 | async-start | bytes 589824 | tf_op jit(solution)/shard_map/all_to_all | solution.py:175
  96.9 7.0 %collective-permute-start.6 = (bf16[128,3072]{1,0:T(8,128)(2,1)S(1)}, bf16[128,3072]{1,0:T(8,128)(2,1)S(1)}, u32[]{:S(2)}, u32[]{:S(2)}) collective-permute-start(bf16[128,3072]{1,0:T(8,128)(2,1)S(1)} %get-tuple-element.22), channel_id=1, source_target_pairs={{0,48},{48,0},{1,49},{49,1},{2,50},{50,2},{3,51},{51,3},{4,52},{52... | collective-permute-start | bytes 2359304 | tf_op jit(solution)/shard_map/ppermute | solution.py:222

commit v4 on v3

--- a/solution.py
+++ b/solution.py
@@ -13,6 +13,7 @@
 SHARD = DIN // (X * YH * CORE)
 PEERS = X * CORE
 HALF = DIN // CORE
+SOME = TOK // CORE
 PIECES = YH * ZL * YL
 ROWS = SHARD // (ZL * YL)
 LANES = 128
@@ -29,9 +30,9 @@
 bf16, f16, f32 = jnp.bfloat16, jnp.float16, jnp.float32
 
 
-def pack_kernel(place, counts, acts, cot, packed, masked, lend, raw, kept, full, built, loan, sems):
+def pack_kernel(x_ref, core_ref, counts, acts, cot, packed, masked, lend, raw, kept, full, built, loan, sems):
     wide = DIN // X
-    away = 1 - place[0]
+    away = 1 - core_ref[0]
     first = pltpu.make_async_copy(cot, raw, sems.at[0])
     first.start()
     loads = [
@@ -53,7 +54,7 @@
             for yh in range(YH):
                 b = (x * YH + yh) * CORE + side
                 built[peer, 0:TOK, yh * SHARD:(yh + 1) * SHARD] = full[:, b * SHARD:(b + 1) * SHARD]
-            built[peer, TOK:2 * TOK, :] = kept[...]
+            built[peer, TOK:TOK + SOME, :] = kept[side * SOME:(side + 1) * SOME, :]
         for yh in range(YH):
             start = pl.multiple_of(((x * YH + yh) * CORE + away) * SHARD, SHARD)
             loan[:, (x * YH + yh) * SHARD:(x * YH + yh + 1) * SHARD] = full[:, pl.ds(start, SHARD)]
@@ -82,13 +83,18 @@
     return ref[i, 0:FLAT, :] * jnp.exp2(-ref[i, FLAT:FLAT + 1, :])
 
 
-def grad_kernel(got, pair, loan, out, same, same_loan, acc):
+def grad_kernel(core_ref, got, rest, pair, loan, out, same, same_loan, right, acc):
+    core = core_ref[0]
+    for i in range(PEERS):
+        near = pl.multiple_of(i * TOK + core * SOME, SOME)
+        far = pl.multiple_of(i * TOK + (1 - core) * SOME, SOME)
+        right[pl.ds(near, SOME), :] = got[i, TOK:TOK + SOME, :]
+        right[pl.ds(far, SOME), :] = rest[i]
     cols = 128
-    right = got[:, TOK:2 * TOK, :].reshape(PEERS * TOK, HD)
     for i in range(YH * SHARD // cols):
         left = got[:, 0:TOK, i * cols:(i + 1) * cols].reshape(PEERS * TOK, cols)
         acc[i * cols:(i + 1) * cols, :] = lax.dot_general(
-            left, right, (((0,), (0,)), ((), ())), preferred_element_type=f32)
+            left, right[...], (((0,), (0,)), ((), ())), preferred_element_type=f32)
     power = exponent(acc[...])
     factor = jnp.exp2(power)
     for i in range(PIECES):
@@ -122,8 +128,8 @@
             out[i * ROWS:(i + 1) * ROWS, j * LANES:(j + 1) * LANES] = value[j * ROWS:(j + 1) * ROWS, :]
 
 
-def project_kernel(place, acts, masked, loan, after, w0, w1, w2, w3, part, grad, grad_away):
-    x, core = place[0], place[1]
+def project_kernel(x_ref, core_ref, acts, masked, loan, after, w0, w1, w2, w3, part, grad, grad_away):
+    x, core = x_ref[0], core_ref[0]
     kept = jnp.concatenate([masked[...], loan[:, HALF:HALF + HD]], axis=0)
     total = jnp.zeros((2 * TOK, HD), f32)
     for k, shards in enumerate((w0, w1, w2, w3)):
@@ -144,8 +150,8 @@
     grad_away[:, HALF + HD:HALF + 2 * HD] = (total[TOK:2 * TOK] - top.astype(f32)).astype(bf16)
 
 
-def join_kernel(place, counts, part, grad, grad_away, projected, act_grad):
-    x, core = place[0], place[1]
+def join_kernel(x_ref, core_ref, counts, part, grad, grad_away, projected, act_grad):
+    x, core = x_ref[0], core_ref[0]
     rows = lax.broadcasted_iota(jnp.int32, (TOK, HD), 0)
     top = grad_away[:, HALF:HALF + HD].astype(f32)
     rest = grad_away[:, HALF + HD:HALF + 2 * HD].astype(f32)
@@ -182,13 +188,14 @@
 
     packed, masked, lend = call(
         pack_kernel,
-        (sds((PEERS, 2 * TOK, HD), bf16), sds((TOK, HD), bf16), sds((TOK, HALF + HD), bf16)),
-        [SMEM, SMEM, ANY, ANY], (ANY, ANY, ANY),
+        (sds((PEERS, TOK + SOME, HD), bf16), sds((TOK, HD), bf16), sds((TOK, HALF + HD), bf16)),
+        [SMEM, SMEM, SMEM, ANY, ANY], (ANY, ANY, ANY),
         (pltpu.VMEM((TOK, HD), bf16), pltpu.VMEM((TOK, HD), bf16), pltpu.VMEM((TOK, DIN), bf16),
-         pltpu.VMEM((PEERS, 2 * TOK, HD), bf16), pltpu.VMEM((TOK, HALF + HD), bf16), dma((3 + 2 * X,))),
+         pltpu.VMEM((PEERS, TOK + SOME, HD), bf16), pltpu.VMEM((TOK, HALF + HD), bf16), dma((3 + 2 * X,))),
         "pack", LARGE,
-    )(core.reshape(1), batch_counts, acts, cotangent)
+    )(x.reshape(1), core.reshape(1), batch_counts, acts, cotangent)
     got = exchange(packed, ("x", "core"))
+    rest = lax.ppermute(got[:, TOK:TOK + SOME, :], "core", SWAP)
 
     near = lax.ppermute(kv_weight, ("yh", "yl"), [(4, 3), (7, 0), (3, 4), (0, 7)])
     far = lax.ppermute(kv_weight, ("yh", "yl"), [(4, 2), (7, 1), (3, 5), (0, 6)])
@@ -199,9 +206,10 @@
     partial, pair, loan = call(
         grad_kernel,
         (sds((PIECES, TALL, LANES), f32), sds((YH, SHARD, HD), bf16), sds((TOK, HALF + HD), bf16)),
-        [VMEM, ANY, ANY], (VMEM, ANY, ANY), (pltpu.VMEM((YH * SHARD, HD), f32),), "grad",
-        input_output_aliases={1: 1, 2: 2},
-    )(got, pair, loan)
+        [SMEM, VMEM, VMEM, ANY, ANY], (VMEM, ANY, ANY),
+        (pltpu.VMEM((PEERS * TOK, HD), bf16), pltpu.VMEM((YH * SHARD, HD), f32)), "grad",
+        input_output_aliases={3: 1, 4: 2},
+    )(core.reshape(1), got, rest, pair, loan)
 
     parts = exchange(partial.astype(f16), ("yh", "zl", "yl"))
     turned = [lax.ppermute(pair, "x", [(i, (i + k) % X) for i in range(X)]) for k in range(1, X)]
@@ -211,19 +219,18 @@
         final_kernel, sds((ZL * YL, TALL, LANES), f32), [VMEM], VMEM, name="final", limit=TINY)(pieces)
     whole = exchange(ready.astype(f16), ("zl", "yl"))
 
-    place = jnp.stack([x, core])
     part, grad, grad_away = call(
         project_kernel,
         (sds((TOK, HD), f32), sds((TOK, HALF), bf16), sds((TOK, HALF + 2 * HD), bf16)),
-        [SMEM, VMEM, VMEM, VMEM, ANY] + [VMEM] * 4, (VMEM,) * 3, (), "project", SMALL,
+        [SMEM, SMEM, VMEM, VMEM, VMEM, ANY] + [VMEM] * 4, (VMEM,) * 3, (), "project", SMALL,
         cost_estimate=pl.CostEstimate(
             flops=4 * TOK * DIN * HD, bytes_accessed=2 * (2 * TOK * DIN + DIN * HD), transcendentals=0),
-    )(place, acts, masked, loan, piece, pair, *turned)
+    )(x.reshape(1), core.reshape(1), acts, masked, loan, piece, pair, *turned)
     grad_away = lax.ppermute(grad_away, "core", SWAP)
     projected, act_grad = call(
         join_kernel, (sds((TOK, HD), bf16), sds((TOK, DIN), bf16)),
-        [SMEM, SMEM] + [VMEM] * 3, (VMEM, VMEM), (), "join", SMALL,
-    )(place, batch_counts, part, grad, grad_away)
+        [SMEM, SMEM, SMEM] + [VMEM] * 3, (VMEM, VMEM), (), "join", SMALL,
+    )(x.reshape(1), core.reshape(1), batch_counts, part, grad, grad_away)
 
     weight_grad = call(
         unpack_kernel, sds((SHARD, HD), f32), [VMEM], VMEM, name="unpack", limit=TINY)(whole.astype(f32))

time: 107 us -> 106 us (level)
  blocking collectives: 0 us -> 17.8 us
  waiting for transfers between devices: 41.8 us -> 31.1 us
  starting transfers between devices: 51.5 us -> 43.3 us
  Pallas kernels: 9.64 us -> 8.17 us
    all_to_all x0 -> x1, blocking collectives: none -> 17.8 us  [exchange(): return lax.all_to_all(value, axes, 0, 0, tiled=True)]
    all_to_all x4 -> x3, starting transfers between devices: 33.4 us -> 22.4 us  [exchange(): return lax.all_to_all(value, axes, 0, 0, tiled=True)]
    ppermute x1, waiting for transfers between devices: 5.62 us -> 0.01 us  [per_device(): lax.ppermute(kv_weight, ('yh', 'yl'), [(4, 3), (7, 0), (3, 4), (0, 7)])]
    ppermute x1, waiting for transfers between devices: 3.64 us -> 0.01 us  [per_device(): lax.ppermute(kv_weight, ('yh', 'yl'), [(4, 2), (7, 1), (3, 5), (0, 6)])]
    all_to_all x4 -> x3, waiting for transfers between devices: 30.7 us -> 27.6 us  [exchange(): return lax.all_to_all(value, axes, 0, 0, tiled=True)]
    ppermute x0 -> x1, starting transfers between devices: none -> 2.77 us  [per_device(): rest = lax.ppermute(got[:, TOK:TOK + SOME, :], 'core', SWAP)]
    ppermute x0 -> x1, waiting for transfers between devices: none -> 1.55 us  [per_device(): rest = lax.ppermute(got[:, TOK:TOK + SOME, :], 'core', SWAP)]
  transfers between devices with their start and end apart: 11 -> 11, of which waited for: 6 -> 4; matrix products, arithmetic and copies ran while one was open for 1% -> 2% of each run, Pallas kernels for 5% -> 4%
where the time goes in v4:
time: 106 us; the launch traced here: 105 us
  starting transfers between devices  43.3 us (41%)
  waiting for transfers between devices  31.1 us (29%)
  blocking collectives  17.8 us (17%)
  Pallas kernels  8.17 us (8%)
  other arithmetic  1.88 us (2%)
  between operations  1.53 us (1%)
    all_to_all x3, waiting for transfers between devices, exchange(): return lax.all_to_all(value, axes, 0, 0, tiled=True)  27.6 us
    all_to_all x3, starting transfers between devices, exchange(): return lax.all_to_all(value, axes, 0, 0, tiled=True)  22.4 us
    all_to_all x1, blocking collectives, exchange(): return lax.all_to_all(value, axes, 0, 0, tiled=True)  17.8 us
    ppermute x3, starting transfers between devices, per_device(): lax.ppermute(pair, 'x', [(i, (i + k) % X) for i in range(X)])  7.81 us
    ppermute x1, starting transfers between devices, per_device(): grad_away = lax.ppermute(grad_away, 'core', SWAP)  5.08 us
    ppermute x1, starting transfers between devices, per_device(): rest = lax.ppermute(got[:, TOK:TOK + SOME, :], 'core', SWAP)  2.77 us
    pallas_call x1, Pallas kernels, per_device(): call(pack_kernel, (sds((PEERS, TOK + SOME, HD), bf16), sds((TOK, HD), bf1...  2.5 us
    pallas_call x1, Pallas kernels, per_device(): call(project_kernel, (sds((TOK, HD), f32), sds((TOK, HALF), bf16), sds((T...  2.48 us
  transfers between devices with their start and end apart: 11, of which 4 were waited for; matrix products, arithmetic and copies ran while one was open for 2% of the time, Pallas kernels for 4%

profile of v4, /device:TPU:1, one launch (start us, length us, event | category | flops | bytes accessed | tf_op | source)
XLA Modules:
  0.0 104.6 jit_solution(13823432937415524666)
XLA Ops:
  1.3 2.5 %pack.1 = (bf16[8,192,512]{2,1,0:T(8,128)(2,1)}, bf16[128,512]{1,0:T(8,128)(2,1)}, bf16[128,2560]{1,0:T(8,128)(2,1)}) custom-call(s32[1]{0:T(128)} %bitcast.x_ref, s32[1]{0:T(128)} %bitcast.1.core_ref, s32[1]{0:T(128)S(6)} %copy.11.counts, bf16[128,4096]{1,0:T(8,128)(2,1)} %acts.3, bf16[128,512]{1,0:T(8,128)(2,1)} %cot.1), custom_call_target="tpu_custom_call" | custom-call | tf_op jit(solution)/shard_map/pack/pallas_call | solution.py:189
  3.8 14.1 %all-to-all-start = ((bf16[8,192,512]{2,1,0:T(8,128)(2,1)}), bf16[8,192,512]{2,1,0:T(8,128)(2,1)S(1)}, u32[]{:S(2)}, u32[]{:S(2)}) async-start(bf16[8,192,512]{2,1,0:T(8,128)(2,1)} %get-tuple-element.15), calls=%async_computation | async-start | bytes 3145728 | tf_op jit(solution)/shard_map/all_to_all | solution.py:181
  17.9 2.0 %collective-permute-start.3 = (bf16[128,2560]{1,0:T(8,128)(2,1)}, bf16[128,2560]{1,0:T(8,128)(2,1)S(1)}, u32[]{:S(2)}, u32[]{:S(2)}) collective-permute-start(bf16[128,2560]{1,0:T(8,128)(2,1)} %get-tuple-element.16), channel_id=1, source_target_pairs={{0,48},{48,0},{1,49},{49,1},{2,50},{50,2},{3,51},{51,3},{4,52},{52... | collective-permute-start | bytes 1966088 | tf_op jit(solution)/shard_map/ppermute | solution.py:204
  20.0 1.3 %collective-permute-start.2 = (bf16[256,512]{1,0:T(8,128)(2,1)S(1)}, bf16[256,512]{1,0:T(8,128)(2,1)S(1)}, u32[]{:S(2)}, u32[]{:S(2)}) collective-permute-start(bf16[256,512]{1,0:T(8,128)(2,1)S(1)} %copy-done.2), channel_id=1, source_target_pairs={{96,2},{99,1},{3,97},{0,98},{100,6},{103,5},{7,101},{4,102},{104,1... | collective-permute-start | bytes 786440 | tf_op jit(solution)/shard_map/ppermute | solution.py:201
  21.3 1.9 %collective-permute-start.1 = (bf16[256,512]{1,0:T(8,128)(2,1)S(1)}, bf16[256,512]{1,0:T(8,128)(2,1)S(1)}, u32[]{:S(2)}, u32[]{:S(2)}) collective-permute-start(bf16[256,512]{1,0:T(8,128)(2,1)S(1)} %copy-done.2), channel_id=1, source_target_pairs={{96,3},{99,0},{3,96},{0,99},{100,7},{103,4},{7,100},{4,103},{104,1... | collective-permute-start | bytes 786440 | tf_op jit(solution)/shard_map/ppermute | solution.py:200
  23.2 15.5 %all-to-all-done.got = bf16[8,192,512]{2,1,0:T(8,128)(2,1)S(1)} async-done(((bf16[8,192,512]{2,1,0:T(8,128)(2,1)}), bf16[8,192,512]{2,1,0:T(8,128)(2,1)S(1)}, u32[]{:S(2)}, u32[]{:S(2)}) %all-to-all-start) | async-done | bytes 1572896 | tf_op jit(solution)/shard_map/all_to_all | solution.py:181
  38.7 0.8 slice.4
  39.5 2.8 %collective-permute-start = (bf16[8,64,512]{2,1,0:T(8,128)(2,1)}, bf16[8,64,512]{2,1,0:T(8,128)(2,1)S(1)}, u32[]{:S(2)}, u32[]{:S(2)}) collective-permute-start(bf16[8,64,512]{2,1,0:T(8,128)(2,1)} %slice.4), channel_id=1, source_target_pairs={{0,48},{48,0},{1,49},{49,1},{2,50},{50,2},{3,51},{51,3},{4,52},{52... | collective-permute-start | bytes 1572872 | tf_op jit(solution)/shard_map/ppermute | solution.py:198
  42.5 1.6 %collective-permute-done.rest = bf16[8,64,512]{2,1,0:T(8,128)(2,1)S(1)} collective-permute-done((bf16[8,64,512]{2,1,0:T(8,128)(2,1)}, bf16[8,64,512]{2,1,0:T(8,128)(2,1)S(1)}, u32[]{:S(2)}, u32[]{:S(2)}) %collective-permute-start) | collective-permute-done | bytes 524320 | tf_op jit(solution)/shard_map/ppermute | solution.py:198
  44.0 1.0 grad.1
  45.0 0.9 convert_element_type.12
  45.9 4.4 %all-to-all-start.1 = ((f16[32,72,128]{2,1,0:T(8,128)(2,1)}), f16[32,72,128]{2,1,0:T(8,128)(2,1)S(1)}, u32[]{:S(2)}, u32[]{:S(2)}) async-start(f16[32,72,128]{2,1,0:T(8,128)(2,1)} %convert_element_type.12), calls=%async_computation.1 | async-start | bytes 1179648 | tf_op jit(solution)/shard_map/all_to_all | solution.py:181
  50.3 2.8 %collective-permute-start.6 = (bf16[2,256,512]{2,1,0:T(8,128)(2,1)S(1)}, bf16[2,256,512]{2,1,0:T(8,128)(2,1)S(1)}, u32[]{:S(2)}, u32[]{:S(2)}) collective-permute-start(bf16[2,256,512]{2,1,0:T(8,128)(2,1)S(1)} %get-tuple-element.19.w0), channel_id=1, source_target_pairs={{0,576},{192,0},{384,192},{576,384},{1,577},{193,1},{385,193},{577... | collective-permute-start | bytes 1572872 | tf_op jit(solution)/shard_map/ppermute | solution.py:215
  53.1 3.1 %collective-permute-start.5 = (bf16[2,256,512]{2,1,0:T(8,128)(2,1)S(1)}, bf16[2,256,512]{2,1,0:T(8,128)(2,1)}, u32[]{:S(2)}, u32[]{:S(2)}) collective-permute-start(bf16[2,256,512]{2,1,0:T(8,128)(2,1)S(1)} %get-tuple-element.19.w0), channel_id=1, source_target_pairs={{0,384},{192,576},{384,0},{576,192},{1,385},{193,577},{385,1},{577... | collective-permute-start | bytes 1572872 | tf_op jit(solution)/shard_map/ppermute | solution.py:215
  56.2 1.9 %collective-permute-start.4 = (bf16[2,256,512]{2,1,0:T(8,128)(2,1)S(1)}, bf16[2,256,512]{2,1,0:T(8,128)(2,1)}, u32[]{:S(2)}, u32[]{:S(2)}) collective-permute-start(bf16[2,256,512]{2,1,0:T(8,128)(2,1)S(1)} %get-tuple-element.19.w0), channel_id=1, source_target_pairs={{0,192},{192,384},{384,576},{576,0},{1,193},{193,385},{385,577},{5... | collective-permute-start | bytes 1572872 | tf_op jit(solution)/shard_map/ppermute | solution.py:215
  58.2 12.2 %all-to-all-done.1 = f16[32,72,128]{2,1,0:T(8,128)(2,1)S(1)} async-done(((f16[32,72,128]{2,1,0:T(8,128)(2,1)}), f16[32,72,128]{2,1,0:T(8,128)(2,1)S(1)}, u32[]{:S(2)}, u32[]{:S(2)}) %all-to-all-start.1) | async-done | bytes 589856 | tf_op jit(solution)/shard_map/all_to_all | solution.py:181
  70.6 17.8 %all_to_all.20.parts = f32[3,64,128]{2,1,0:T(8,128)S(1)} all-to-all(f32[3,64,128]{2,1,0:T(8,128)S(1)} %sum.1.after), channel_id=1, replica_groups=mesh['x'=4,'yh'=2,'core'=2,'zh'=3,'zl'=4,'yl'=4] {'zh'}, dimensions={0} | all-to-all | bytes 196608 | tf_op jit(solution)/shard_map/all_to_all | solution.py:181
  88.5 0.8 convert_element_type.14
  89.2 3.9 %all-to-all-start.3 = ((f16[16,72,128]{2,1,0:T(8,128)(2,1)}), f16[16,72,128]{2,1,0:T(8,128)(2,1)S(1)}, u32[]{:S(2)}, u32[]{:S(2)}) async-start(f16[16,72,128]{2,1,0:T(8,128)(2,1)} %convert_element_type.14), calls=%async_computation.3 | async-start | bytes 589824 | tf_op jit(solution)/shard_map/all_to_all | solution.py:181
  93.1 2.5 %project.1 = (f32[128,512]{1,0:T(8,128)S(1)}, bf16[128,2048]{1,0:T(8,128)(2,1)S(1)}, bf16[128,3072]{1,0:T(8,128)(2,1)S(1)}) custom-call(s32[1]{0:T(128)} %bitcast.x_ref, s32[1]{0:T(128)} %bitcast.1.core_ref, bf16[128,4096]{1,0:T(8,128)(2,1)S(1)} %copy-done, bf16[128,512]{1,0:T(8,128)(2,1)S(1)} %copy-done.1, bf16[128,2560]{1,0:T(8,128)(2,1)S(1)} %get-tuple-element.17.loan, ...), custom_call_target="tpu_custom_call" | custom-call | flops 1073741824 | bytes 6291456 | tf_op jit(solution)/shard_map/project/pallas_call | solution.py:222
  95.6 5.1 %collective-permute-start.7 = (bf16[128,3072]{1,0:T(8,128)(2,1)S(1)}, bf16[128,3072]{1,0:T(8,128)(2,1)S(1)}, u32[]{:S(2)}, u32[]{:S(2)}) collective-permute-start(bf16[128,3072]{1,0:T(8,128)(2,1)S(1)} %get-tuple-element.22), channel_id=1, source_target_pairs={{0,48},{48,0},{1,49},{49,1},{2,50},{50,2},{3,51},{51,3},{4,52},{52... | collective-permute-start | bytes 2359304 | tf_op jit(solution)/shard_map/ppermute | solution.py:229
  100.7 1.9 %collective-permute-done.7.grad_away = bf16[128,3072]{1,0:T(8,128)(2,1)S(1)} collective-permute-done((bf16[128,3072]{1,0:T(8,128)(2,1)S(1)}, bf16[128,3072]{1,0:T(8,128)(2,1)S(1)}, u32[]{:S(2)}, u32[]{:S(2)}) %collective-permute-start.7) | collective-permute-done | bytes 786464 | tf_op jit(solution)/shard_map/ppermute | solution.py:229
  102.6 1.1 %join.1 = (bf16[128,512]{1,0:T(8,128)(2,1)}, bf16[128,4096]{1,0:T(8,128)(2,1)}) custom-call(s32[1]{0:T(128)} %bitcast.x_ref, s32[1]{0:T(128)} %bitcast.1.core_ref, s32[1]{0:T(128)S(6)} %copy.11.counts, f32[128,512]{1,0:T(8,128)S(1)} %get-tuple-element.20.part, bf16[128,2048]{1,0:T(8,128)(2,1)S(1)} %get-tuple-element.21.grad, ...), custom_call_target="tpu_custom_call" | custom-call | tf_op jit(solution)/shard_map/join/pallas_call | solution.py:230
  103.8 0.8 unpack.1
  (19 shorter events, 0.5 us)
Async XLA Ops:
  3.8 16.2 %copy-start.2 = (bf16[256,512]{1,0:T(8,128)(2,1)S(1)}, bf16[256,512]{1,0:T(8,128)(2,1)}, u32[]{:S(2)}) copy-start(bf16[256,512]{1,0:T(8,128)(2,1)} %param.6) | copy-start | bytes 786436
  3.8 34.9 %all-to-all-start = ((bf16[8,192,512]{2,1,0:T(8,128)(2,1)}), bf16[8,192,512]{2,1,0:T(8,128)(2,1)S(1)}, u32[]{:S(2)}, u32[]{:S(2)}) async-start(bf16[8,192,512]{2,1,0:T(8,128)(2,1)} %get-tuple-element.15), calls=%async_computation | async-start | bytes 3145728 | tf_op jit(solution)/shard_map/all_to_all | solution.py:181
  17.9 24.5 %collective-permute-start.3 = (bf16[128,2560]{1,0:T(8,128)(2,1)}, bf16[128,2560]{1,0:T(8,128)(2,1)S(1)}, u32[]{:S(2)}, u32[]{:S(2)}) collective-permute-start(bf16[128,2560]{1,0:T(8,128)(2,1)} %get-tuple-element.16), channel_id=1, source_target_pairs={{0,48},{48,0},{1,49},{49,1},{2,50},{50,2},{3,51},{51,3},{4,52},{52... | collective-permute-start | bytes 1966088 | tf_op jit(solution)/shard_map/ppermute | solution.py:204
  20.0 22.3 %collective-permute-start.2 = (bf16[256,512]{1,0:T(8,128)(2,1)S(1)}, bf16[256,512]{1,0:T(8,128)(2,1)S(1)}, u32[]{:S(2)}, u32[]{:S(2)}) collective-permute-start(bf16[256,512]{1,0:T(8,128)(2,1)S(1)} %copy-done.2), channel_id=1, source_target_pairs={{96,2},{99,1},{3,97},{0,98},{100,6},{103,5},{7,101},{4,102},{104,1... | collective-permute-start | bytes 786440 | tf_op jit(solution)/shard_map/ppermute | solution.py:201
  21.3 21.0 %collective-permute-start.1 = (bf16[256,512]{1,0:T(8,128)(2,1)S(1)}, bf16[256,512]{1,0:T(8,128)(2,1)S(1)}, u32[]{:S(2)}, u32[]{:S(2)}) collective-permute-start(bf16[256,512]{1,0:T(8,128)(2,1)S(1)} %copy-done.2), channel_id=1, source_target_pairs={{96,3},{99,0},{3,96},{0,99},{100,7},{103,4},{7,100},{4,103},{104,1... | collective-permute-start | bytes 786440 | tf_op jit(solution)/shard_map/ppermute | solution.py:200
  39.5 4.5 %collective-permute-start = (bf16[8,64,512]{2,1,0:T(8,128)(2,1)}, bf16[8,64,512]{2,1,0:T(8,128)(2,1)S(1)}, u32[]{:S(2)}, u32[]{:S(2)}) collective-permute-start(bf16[8,64,512]{2,1,0:T(8,128)(2,1)} %slice.4), channel_id=1, source_target_pairs={{0,48},{48,0},{1,49},{49,1},{2,50},{50,2},{3,51},{51,3},{4,52},{52... | collective-permute-start | bytes 1572872 | tf_op jit(solution)/shard_map/ppermute | solution.py:198
  45.9 24.4 %all-to-all-start.1 = ((f16[32,72,128]{2,1,0:T(8,128)(2,1)}), f16[32,72,128]{2,1,0:T(8,128)(2,1)S(1)}, u32[]{:S(2)}, u32[]{:S(2)}) async-start(f16[32,72,128]{2,1,0:T(8,128)(2,1)} %convert_element_type.12), calls=%async_computation.1 | async-start | bytes 1179648 | tf_op jit(solution)/shard_map/all_to_all | solution.py:181
  50.3 42.8 %collective-permute-start.6 = (bf16[2,256,512]{2,1,0:T(8,128)(2,1)S(1)}, bf16[2,256,512]{2,1,0:T(8,128)(2,1)S(1)}, u32[]{:S(2)}, u32[]{:S(2)}) collective-permute-start(bf16[2,256,512]{2,1,0:T(8,128)(2,1)S(1)} %get-tuple-element.19.w0), channel_id=1, source_target_pairs={{0,576},{192,0},{384,192},{576,384},{1,577},{193,1},{385,193},{577... | collective-permute-start | bytes 1572872 | tf_op jit(solution)/shard_map/ppermute | solution.py:215
  53.1 40.0 %collective-permute-start.5 = (bf16[2,256,512]{2,1,0:T(8,128)(2,1)S(1)}, bf16[2,256,512]{2,1,0:T(8,128)(2,1)}, u32[]{:S(2)}, u32[]{:S(2)}) collective-permute-start(bf16[2,256,512]{2,1,0:T(8,128)(2,1)S(1)} %get-tuple-element.19.w0), channel_id=1, source_target_pairs={{0,384},{192,576},{384,0},{576,192},{1,385},{193,577},{385,1},{577... | collective-permute-start | bytes 1572872 | tf_op jit(solution)/shard_map/ppermute | solution.py:215
  56.2 36.9 %collective-permute-start.4 = (bf16[2,256,512]{2,1,0:T(8,128)(2,1)S(1)}, bf16[2,256,512]{2,1,0:T(8,128)(2,1)}, u32[]{:S(2)}, u32[]{:S(2)}) collective-permute-start(bf16[2,256,512]{2,1,0:T(8,128)(2,1)S(1)} %get-tuple-element.19.w0), channel_id=1, source_target_pairs={{0,192},{192,384},{384,576},{576,0},{1,193},{193,385},{385,577},{5... | collective-permute-start | bytes 1572872 | tf_op jit(solution)/shard_map/ppermute | solution.py:215
  70.4 22.7 %copy-start = (bf16[128,4096]{1,0:T(8,128)(2,1)S(1)}, bf16[128,4096]{1,0:T(8,128)(2,1)}, u32[]{:S(2)}) copy-start(bf16[128,4096]{1,0:T(8,128)(2,1)} %acts.3) | copy-start | bytes 3145732
  70.4 22.7 %copy-start.1 = (bf16[128,512]{1,0:T(8,128)(2,1)S(1)}, bf16[128,512]{1,0:T(8,128)(2,1)}, u32[]{:S(2)}) copy-start(bf16[128,512]{1,0:T(8,128)(2,1)} %get-tuple-element.14.masked) | copy-start | bytes 393220
  89.2 14.5 %all-to-all-start.3 = ((f16[16,72,128]{2,1,0:T(8,128)(2,1)}), f16[16,72,128]{2,1,0:T(8,128)(2,1)S(1)}, u32[]{:S(2)}, u32[]{:S(2)}) async-start(f16[16,72,128]{2,1,0:T(8,128)(2,1)} %convert_element_type.14), calls=%async_computation.3 | async-start | bytes 589824 | tf_op jit(solution)/shard_map/all_to_all | solution.py:181
  95.6 7.0 %collective-permute-start.7 = (bf16[128,3072]{1,0:T(8,128)(2,1)S(1)}, bf16[128,3072]{1,0:T(8,128)(2,1)S(1)}, u32[]{:S(2)}, u32[]{:S(2)}) collective-permute-start(bf16[128,3072]{1,0:T(8,128)(2,1)S(1)} %get-tuple-element.22), channel_id=1, source_target_pairs={{0,48},{48,0},{1,49},{49,1},{2,50},{50,2},{3,51},{51,3},{4,52},{52... | collective-permute-start | bytes 2359304 | tf_op jit(solution)/shard_map/ppermute | solution.py:229

commit v5 on v4

--- a/solution.py
+++ b/solution.py
@@ -83,18 +83,23 @@
     return ref[i, 0:FLAT, :] * jnp.exp2(-ref[i, FLAT:FLAT + 1, :])
 
 
-def grad_kernel(core_ref, got, rest, pair, loan, out, same, same_loan, right, acc):
-    core = core_ref[0]
-    for i in range(PEERS):
-        near = pl.multiple_of(i * TOK + core * SOME, SOME)
-        far = pl.multiple_of(i * TOK + (1 - core) * SOME, SOME)
-        right[pl.ds(near, SOME), :] = got[i, TOK:TOK + SOME, :]
-        right[pl.ds(far, SOME), :] = rest[i]
+def half_grad(got, rows, core, acc, first):
     cols = 128
+    start = pl.multiple_of(core * SOME, SOME)
+    right = rows.reshape(PEERS * SOME, HD)
     for i in range(YH * SHARD // cols):
-        left = got[:, 0:TOK, i * cols:(i + 1) * cols].reshape(PEERS * TOK, cols)
-        acc[i * cols:(i + 1) * cols, :] = lax.dot_general(
-            left, right[...], (((0,), (0,)), ((), ())), preferred_element_type=f32)
+        left = got[:, pl.ds(start, SOME), i * cols:(i + 1) * cols].reshape(PEERS * SOME, cols)
+        part = lax.dot_general(left, right, (((0,), (0,)), ((), ())), preferred_element_type=f32)
+        span = slice(i * cols, (i + 1) * cols)
+        acc[span, :] = part + first[span, :] if first is not None else part
+
+
+def near_kernel(core_ref, got, acc):
+    half_grad(got, got[:, TOK:TOK + SOME, :], core_ref[0], acc, None)
+
+
+def grad_kernel(core_ref, got, first, rest, pair, loan, out, same, same_loan, acc):
+    half_grad(got, rest[...], 1 - core_ref[0], acc, first)
     power = exponent(acc[...])
     factor = jnp.exp2(power)
     for i in range(PIECES):
@@ -203,13 +208,14 @@
     pair = jnp.where(yh == 0, jnp.stack([kv_weight, twin]), jnp.stack([twin, kv_weight]))
     loan = lax.ppermute(lend, "core", SWAP)
 
+    first = call(near_kernel, sds((YH * SHARD, HD), f32), [SMEM, VMEM], VMEM, name="near")(core.reshape(1), got)
     partial, pair, loan = call(
         grad_kernel,
         (sds((PIECES, TALL, LANES), f32), sds((YH, SHARD, HD), bf16), sds((TOK, HALF + HD), bf16)),
-        [SMEM, VMEM, VMEM, ANY, ANY], (VMEM, ANY, ANY),
-        (pltpu.VMEM((PEERS * TOK, HD), bf16), pltpu.VMEM((YH * SHARD, HD), f32)), "grad",
-        input_output_aliases={3: 1, 4: 2},
-    )(core.reshape(1), got, rest, pair, loan)
+        [SMEM, VMEM, VMEM, VMEM, ANY, ANY], (VMEM, ANY, ANY),
+        (pltpu.VMEM((YH * SHARD, HD), f32),), "grad",
+        input_output_aliases={4: 1, 5: 2},
+    )(core.reshape(1), got, first, rest, pair, loan)
 
     parts = exchange(partial.astype(f16), ("yh", "zl", "yl"))
     turned = [lax.ppermute(pair, "x", [(i, (i + k) % X) for i in range(X)]) for k in range(1, X)]

time: 106 us -> 105 us (level)
  no operation moved by 1% of the time
where the time goes in v5:
time: 105 us; the launch traced here: 104 us
  starting transfers between devices  43.3 us (41%)
  waiting for transfers between devices  30.6 us (29%)
  blocking collectives  17.8 us (17%)
  Pallas kernels  8.31 us (8%)
  other arithmetic  1.88 us (2%)
  between operations  1.54 us (1%)
    all_to_all x3, waiting for transfers between devices, exchange(): return lax.all_to_all(value, axes, 0, 0, tiled=True)  27.6 us
    all_to_all x3, starting transfers between devices, exchange(): return lax.all_to_all(value, axes, 0, 0, tiled=True)  22.4 us
    all_to_all x1, blocking collectives, exchange(): return lax.all_to_all(value, axes, 0, 0, tiled=True)  17.8 us
    ppermute x3, starting transfers between devices, per_device(): lax.ppermute(pair, 'x', [(i, (i + k) % X) for i in range(X)])  7.81 us
    ppermute x1, starting transfers between devices, per_device(): grad_away = lax.ppermute(grad_away, 'core', SWAP)  5.07 us
    ppermute x1, starting transfers between devices, per_device(): rest = lax.ppermute(got[:, TOK:TOK + SOME, :], 'core', SWAP)  2.77 us
    pallas_call x1, Pallas kernels, per_device(): call(pack_kernel, (sds((PEERS, TOK + SOME, HD), bf16), sds((TOK, HD), bf1...  2.5 us
    pallas_call x1, Pallas kernels, per_device(): call(project_kernel, (sds((TOK, HD), f32), sds((TOK, HALF), bf16), sds((T...  2.49 us
  transfers between devices with their start and end apart: 11, of which 4 were waited for; matrix products, arithmetic and copies ran while one was open for 2% of the time, Pallas kernels for 4%

profile of v5, /device:TPU:1, one launch (start us, length us, event | category | flops | bytes accessed | tf_op | source)
XLA Modules:
  0.0 104.3 jit_solution(4498455443252060724)
XLA Ops:
  1.3 2.5 %pack.1 = (bf16[8,192,512]{2,1,0:T(8,128)(2,1)}, bf16[128,512]{1,0:T(8,128)(2,1)}, bf16[128,2560]{1,0:T(8,128)(2,1)}) custom-call(s32[1]{0:T(128)} %bitcast.x_ref, s32[1]{0:T(128)} %bitcast.1.core_ref, s32[1]{0:T(128)S(6)} %copy.11.counts, bf16[128,4096]{1,0:T(8,128)(2,1)} %acts.3, bf16[128,512]{1,0:T(8,128)(2,1)} %cot.1), custom_call_target="tpu_custom_call" | custom-call | tf_op jit(solution)/shard_map/pack/pallas_call | solution.py:194
  3.8 14.1 %all-to-all-start = ((bf16[8,192,512]{2,1,0:T(8,128)(2,1)}), bf16[8,192,512]{2,1,0:T(8,128)(2,1)S(1)}, u32[]{:S(2)}, u32[]{:S(2)}) async-start(bf16[8,192,512]{2,1,0:T(8,128)(2,1)} %get-tuple-element.15), calls=%async_computation | async-start | bytes 3145728 | tf_op jit(solution)/shard_map/all_to_all | solution.py:186
  17.9 2.0 %collective-permute-start.3 = (bf16[128,2560]{1,0:T(8,128)(2,1)}, bf16[128,2560]{1,0:T(8,128)(2,1)S(1)}, u32[]{:S(2)}, u32[]{:S(2)}) collective-permute-start(bf16[128,2560]{1,0:T(8,128)(2,1)} %get-tuple-element.16), channel_id=1, source_target_pairs={{0,48},{48,0},{1,49},{49,1},{2,50},{50,2},{3,51},{51,3},{4,52},{52... | collective-permute-start | bytes 1966088 | tf_op jit(solution)/shard_map/ppermute | solution.py:209
  20.0 1.3 %collective-permute-start.2 = (bf16[256,512]{1,0:T(8,128)(2,1)S(1)}, bf16[256,512]{1,0:T(8,128)(2,1)S(1)}, u32[]{:S(2)}, u32[]{:S(2)}) collective-permute-start(bf16[256,512]{1,0:T(8,128)(2,1)S(1)} %copy-done.2), channel_id=1, source_target_pairs={{96,2},{99,1},{3,97},{0,98},{100,6},{103,5},{7,101},{4,102},{104,1... | collective-permute-start | bytes 786440 | tf_op jit(solution)/shard_map/ppermute | solution.py:206
  21.3 1.9 %collective-permute-start.1 = (bf16[256,512]{1,0:T(8,128)(2,1)S(1)}, bf16[256,512]{1,0:T(8,128)(2,1)S(1)}, u32[]{:S(2)}, u32[]{:S(2)}) collective-permute-start(bf16[256,512]{1,0:T(8,128)(2,1)S(1)} %copy-done.2), channel_id=1, source_target_pairs={{96,3},{99,0},{3,96},{0,99},{100,7},{103,4},{7,100},{4,103},{104,1... | collective-permute-start | bytes 786440 | tf_op jit(solution)/shard_map/ppermute | solution.py:205
  23.2 15.5 %all-to-all-done.got = bf16[8,192,512]{2,1,0:T(8,128)(2,1)S(1)} async-done(((bf16[8,192,512]{2,1,0:T(8,128)(2,1)}), bf16[8,192,512]{2,1,0:T(8,128)(2,1)S(1)}, u32[]{:S(2)}, u32[]{:S(2)}) %all-to-all-start) | async-done | bytes 1572896 | tf_op jit(solution)/shard_map/all_to_all | solution.py:186
  38.7 0.8 slice.4
  39.5 2.8 %collective-permute-start = (bf16[8,64,512]{2,1,0:T(8,128)(2,1)}, bf16[8,64,512]{2,1,0:T(8,128)(2,1)S(1)}, u32[]{:S(2)}, u32[]{:S(2)}) collective-permute-start(bf16[8,64,512]{2,1,0:T(8,128)(2,1)} %slice.4), channel_id=1, source_target_pairs={{0,48},{48,0},{1,49},{49,1},{2,50},{50,2},{3,51},{51,3},{4,52},{52... | collective-permute-start | bytes 1572872 | tf_op jit(solution)/shard_map/ppermute | solution.py:203
  43.0 1.1 %collective-permute-done.rest = bf16[8,64,512]{2,1,0:T(8,128)(2,1)S(1)} collective-permute-done((bf16[8,64,512]{2,1,0:T(8,128)(2,1)}, bf16[8,64,512]{2,1,0:T(8,128)(2,1)S(1)}, u32[]{:S(2)}, u32[]{:S(2)}) %collective-permute-start) | collective-permute-done | bytes 524320 | tf_op jit(solution)/shard_map/ppermute | solution.py:203
  44.0 0.6 grad.1
  44.7 0.9 convert_element_type.12
  45.6 4.4 %all-to-all-start.1 = ((f16[32,72,128]{2,1,0:T(8,128)(2,1)}), f16[32,72,128]{2,1,0:T(8,128)(2,1)S(1)}, u32[]{:S(2)}, u32[]{:S(2)}) async-start(f16[32,72,128]{2,1,0:T(8,128)(2,1)} %convert_element_type.12), calls=%async_computation.1 | async-start | bytes 1179648 | tf_op jit(solution)/shard_map/all_to_all | solution.py:186
  50.0 2.8 %collective-permute-start.6 = (bf16[2,256,512]{2,1,0:T(8,128)(2,1)S(1)}, bf16[2,256,512]{2,1,0:T(8,128)(2,1)S(1)}, u32[]{:S(2)}, u32[]{:S(2)}) collective-permute-start(bf16[2,256,512]{2,1,0:T(8,128)(2,1)S(1)} %get-tuple-element.19.w0), channel_id=1, source_target_pairs={{0,576},{192,0},{384,192},{576,384},{1,577},{193,1},{385,193},{577... | collective-permute-start | bytes 1572872 | tf_op jit(solution)/shard_map/ppermute | solution.py:221
  52.8 3.1 %collective-permute-start.5 = (bf16[2,256,512]{2,1,0:T(8,128)(2,1)S(1)}, bf16[2,256,512]{2,1,0:T(8,128)(2,1)}, u32[]{:S(2)}, u32[]{:S(2)}) collective-permute-start(bf16[2,256,512]{2,1,0:T(8,128)(2,1)S(1)} %get-tuple-element.19.w0), channel_id=1, source_target_pairs={{0,384},{192,576},{384,0},{576,192},{1,385},{193,577},{385,1},{577... | collective-permute-start | bytes 1572872 | tf_op jit(solution)/shard_map/ppermute | solution.py:221
  55.9 1.9 %collective-permute-start.4 = (bf16[2,256,512]{2,1,0:T(8,128)(2,1)S(1)}, bf16[2,256,512]{2,1,0:T(8,128)(2,1)}, u32[]{:S(2)}, u32[]{:S(2)}) collective-permute-start(bf16[2,256,512]{2,1,0:T(8,128)(2,1)S(1)} %get-tuple-element.19.w0), channel_id=1, source_target_pairs={{0,192},{192,384},{384,576},{576,0},{1,193},{193,385},{385,577},{5... | collective-permute-start | bytes 1572872 | tf_op jit(solution)/shard_map/ppermute | solution.py:221
  57.8 12.2 %all-to-all-done.1 = f16[32,72,128]{2,1,0:T(8,128)(2,1)S(1)} async-done(((f16[32,72,128]{2,1,0:T(8,128)(2,1)}), f16[32,72,128]{2,1,0:T(8,128)(2,1)S(1)}, u32[]{:S(2)}, u32[]{:S(2)}) %all-to-all-start.1) | async-done | bytes 589856 | tf_op jit(solution)/shard_map/all_to_all | solution.py:186
  70.2 17.8 %all_to_all.20.parts = f32[3,64,128]{2,1,0:T(8,128)S(1)} all-to-all(f32[3,64,128]{2,1,0:T(8,128)S(1)} %sum.1.after), channel_id=1, replica_groups=mesh['x'=4,'yh'=2,'core'=2,'zh'=3,'zl'=4,'yl'=4] {'zh'}, dimensions={0} | all-to-all | bytes 196608 | tf_op jit(solution)/shard_map/all_to_all | solution.py:186
  88.1 0.8 convert_element_type.14
  88.9 3.9 %all-to-all-start.3 = ((f16[16,72,128]{2,1,0:T(8,128)(2,1)}), f16[16,72,128]{2,1,0:T(8,128)(2,1)S(1)}, u32[]{:S(2)}, u32[]{:S(2)}) async-start(f16[16,72,128]{2,1,0:T(8,128)(2,1)} %convert_element_type.14), calls=%async_computation.3 | async-start | bytes 589824 | tf_op jit(solution)/shard_map/all_to_all | solution.py:186
  92.8 2.5 %project.1 = (f32[128,512]{1,0:T(8,128)S(1)}, bf16[128,2048]{1,0:T(8,128)(2,1)S(1)}, bf16[128,3072]{1,0:T(8,128)(2,1)S(1)}) custom-call(s32[1]{0:T(128)} %bitcast.x_ref, s32[1]{0:T(128)} %bitcast.1.core_ref, bf16[128,4096]{1,0:T(8,128)(2,1)S(1)} %copy-done, bf16[128,512]{1,0:T(8,128)(2,1)S(1)} %copy-done.1, bf16[128,2560]{1,0:T(8,128)(2,1)S(1)} %get-tuple-element.17.loan, ...), custom_call_target="tpu_custom_call" | custom-call | flops 1073741824 | bytes 6291456 | tf_op jit(solution)/shard_map/project/pallas_call | solution.py:228
  95.3 5.1 %collective-permute-start.7 = (bf16[128,3072]{1,0:T(8,128)(2,1)S(1)}, bf16[128,3072]{1,0:T(8,128)(2,1)S(1)}, u32[]{:S(2)}, u32[]{:S(2)}) collective-permute-start(bf16[128,3072]{1,0:T(8,128)(2,1)S(1)} %get-tuple-element.22), channel_id=1, source_target_pairs={{0,48},{48,0},{1,49},{49,1},{2,50},{50,2},{3,51},{51,3},{4,52},{52... | collective-permute-start | bytes 2359304 | tf_op jit(solution)/shard_map/ppermute | solution.py:235
  100.4 1.9 %collective-permute-done.7.grad_away = bf16[128,3072]{1,0:T(8,128)(2,1)S(1)} collective-permute-done((bf16[128,3072]{1,0:T(8,128)(2,1)S(1)}, bf16[128,3072]{1,0:T(8,128)(2,1)S(1)}, u32[]{:S(2)}, u32[]{:S(2)}) %collective-permute-start.7) | collective-permute-done | bytes 786464 | tf_op jit(solution)/shard_map/ppermute | solution.py:235
  102.3 1.1 %join.1 = (bf16[128,512]{1,0:T(8,128)(2,1)}, bf16[128,4096]{1,0:T(8,128)(2,1)}) custom-call(s32[1]{0:T(128)} %bitcast.x_ref, s32[1]{0:T(128)} %bitcast.1.core_ref, s32[1]{0:T(128)S(6)} %copy.11.counts, f32[128,512]{1,0:T(8,128)S(1)} %get-tuple-element.20.part, bf16[128,2048]{1,0:T(8,128)(2,1)S(1)} %get-tuple-element.21.grad, ...), custom_call_target="tpu_custom_call" | custom-call | tf_op jit(solution)/shard_map/join/pallas_call | solution.py:236
  103.5 0.8 unpack.1
  (20 shorter events, 1.0 us)
Async XLA Ops:
  3.8 16.2 %copy-start.2 = (bf16[256,512]{1,0:T(8,128)(2,1)S(1)}, bf16[256,512]{1,0:T(8,128)(2,1)}, u32[]{:S(2)}) copy-start(bf16[256,512]{1,0:T(8,128)(2,1)} %param.6) | copy-start | bytes 786436
  3.8 34.9 %all-to-all-start = ((bf16[8,192,512]{2,1,0:T(8,128)(2,1)}), bf16[8,192,512]{2,1,0:T(8,128)(2,1)S(1)}, u32[]{:S(2)}, u32[]{:S(2)}) async-start(bf16[8,192,512]{2,1,0:T(8,128)(2,1)} %get-tuple-element.15), calls=%async_computation | async-start | bytes 3145728 | tf_op jit(solution)/shard_map/all_to_all | solution.py:186
  17.9 25.0 %collective-permute-start.3 = (bf16[128,2560]{1,0:T(8,128)(2,1)}, bf16[128,2560]{1,0:T(8,128)(2,1)S(1)}, u32[]{:S(2)}, u32[]{:S(2)}) collective-permute-start(bf16[128,2560]{1,0:T(8,128)(2,1)} %get-tuple-element.16), channel_id=1, source_target_pairs={{0,48},{48,0},{1,49},{49,1},{2,50},{50,2},{3,51},{51,3},{4,52},{52... | collective-permute-start | bytes 1966088 | tf_op jit(solution)/shard_map/ppermute | solution.py:209
  20.0 22.3 %collective-permute-start.2 = (bf16[256,512]{1,0:T(8,128)(2,1)S(1)}, bf16[256,512]{1,0:T(8,128)(2,1)S(1)}, u32[]{:S(2)}, u32[]{:S(2)}) collective-permute-start(bf16[256,512]{1,0:T(8,128)(2,1)S(1)} %copy-done.2), channel_id=1, source_target_pairs={{96,2},{99,1},{3,97},{0,98},{100,6},{103,5},{7,101},{4,102},{104,1... | collective-permute-start | bytes 786440 | tf_op jit(solution)/shard_map/ppermute | solution.py:206
  21.3 21.0 %collective-permute-start.1 = (bf16[256,512]{1,0:T(8,128)(2,1)S(1)}, bf16[256,512]{1,0:T(8,128)(2,1)S(1)}, u32[]{:S(2)}, u32[]{:S(2)}) collective-permute-start(bf16[256,512]{1,0:T(8,128)(2,1)S(1)} %copy-done.2), channel_id=1, source_target_pairs={{96,3},{99,0},{3,96},{0,99},{100,7},{103,4},{7,100},{4,103},{104,1... | collective-permute-start | bytes 786440 | tf_op jit(solution)/shard_map/ppermute | solution.py:205
  39.5 4.5 %collective-permute-start = (bf16[8,64,512]{2,1,0:T(8,128)(2,1)}, bf16[8,64,512]{2,1,0:T(8,128)(2,1)S(1)}, u32[]{:S(2)}, u32[]{:S(2)}) collective-permute-start(bf16[8,64,512]{2,1,0:T(8,128)(2,1)} %slice.4), channel_id=1, source_target_pairs={{0,48},{48,0},{1,49},{49,1},{2,50},{50,2},{3,51},{51,3},{4,52},{52... | collective-permute-start | bytes 1572872 | tf_op jit(solution)/shard_map/ppermute | solution.py:203
  45.6 24.4 %all-to-all-start.1 = ((f16[32,72,128]{2,1,0:T(8,128)(2,1)}), f16[32,72,128]{2,1,0:T(8,128)(2,1)S(1)}, u32[]{:S(2)}, u32[]{:S(2)}) async-start(f16[32,72,128]{2,1,0:T(8,128)(2,1)} %convert_element_type.12), calls=%async_computation.1 | async-start | bytes 1179648 | tf_op jit(solution)/shard_map/all_to_all | solution.py:186
  50.0 42.8 %collective-permute-start.6 = (bf16[2,256,512]{2,1,0:T(8,128)(2,1)S(1)}, bf16[2,256,512]{2,1,0:T(8,128)(2,1)S(1)}, u32[]{:S(2)}, u32[]{:S(2)}) collective-permute-start(bf16[2,256,512]{2,1,0:T(8,128)(2,1)S(1)} %get-tuple-element.19.w0), channel_id=1, source_target_pairs={{0,576},{192,0},{384,192},{576,384},{1,577},{193,1},{385,193},{577... | collective-permute-start | bytes 1572872 | tf_op jit(solution)/shard_map/ppermute | solution.py:221
  52.8 40.0 %collective-permute-start.5 = (bf16[2,256,512]{2,1,0:T(8,128)(2,1)S(1)}, bf16[2,256,512]{2,1,0:T(8,128)(2,1)}, u32[]{:S(2)}, u32[]{:S(2)}) collective-permute-start(bf16[2,256,512]{2,1,0:T(8,128)(2,1)S(1)} %get-tuple-element.19.w0), channel_id=1, source_target_pairs={{0,384},{192,576},{384,0},{576,192},{1,385},{193,577},{385,1},{577... | collective-permute-start | bytes 1572872 | tf_op jit(solution)/shard_map/ppermute | solution.py:221
  55.9 36.9 %collective-permute-start.4 = (bf16[2,256,512]{2,1,0:T(8,128)(2,1)S(1)}, bf16[2,256,512]{2,1,0:T(8,128)(2,1)}, u32[]{:S(2)}, u32[]{:S(2)}) collective-permute-start(bf16[2,256,512]{2,1,0:T(8,128)(2,1)S(1)} %get-tuple-element.19.w0), channel_id=1, source_target_pairs={{0,192},{192,384},{384,576},{576,0},{1,193},{193,385},{385,577},{5... | collective-permute-start | bytes 1572872 | tf_op jit(solution)/shard_map/ppermute | solution.py:221
  70.1 22.7 %copy-start = (bf16[128,4096]{1,0:T(8,128)(2,1)S(1)}, bf16[128,4096]{1,0:T(8,128)(2,1)}, u32[]{:S(2)}) copy-start(bf16[128,4096]{1,0:T(8,128)(2,1)} %acts.3) | copy-start | bytes 3145732
  70.1 22.7 %copy-start.1 = (bf16[128,512]{1,0:T(8,128)(2,1)S(1)}, bf16[128,512]{1,0:T(8,128)(2,1)}, u32[]{:S(2)}) copy-start(bf16[128,512]{1,0:T(8,128)(2,1)} %get-tuple-element.14.masked) | copy-start | bytes 393220
  88.9 14.5 %all-to-all-start.3 = ((f16[16,72,128]{2,1,0:T(8,128)(2,1)}), f16[16,72,128]{2,1,0:T(8,128)(2,1)S(1)}, u32[]{:S(2)}, u32[]{:S(2)}) async-start(f16[16,72,128]{2,1,0:T(8,128)(2,1)} %convert_element_type.14), calls=%async_computation.3 | async-start | bytes 589824 | tf_op jit(solution)/shard_map/all_to_all | solution.py:186
  95.3 7.0 %collective-permute-start.7 = (bf16[128,3072]{1,0:T(8,128)(2,1)S(1)}, bf16[128,3072]{1,0:T(8,128)(2,1)S(1)}, u32[]{:S(2)}, u32[]{:S(2)}) collective-permute-start(bf16[128,3072]{1,0:T(8,128)(2,1)S(1)} %get-tuple-element.22), channel_id=1, source_target_pairs={{0,48},{48,0},{1,49},{49,1},{2,50},{50,2},{3,51},{51,3},{4,52},{52... | collective-permute-start | bytes 2359304 | tf_op jit(solution)/shard_map/ppermute | solution.py:235
